TPU v7x, 256 devices: a whole 4x4x8 slice. The times are simulated.
256 devices in a mesh: row: 8 (over z), col: 32 (over x, y, core).
Axes of the slice: x: 4, y: 4, z: 8, core: 2. Of those that a mesh axis runs over, the one named last changes fastest.
Arguments:
- feats: bfloat16 [65536, 256], P(('row', 'col')), may hold values from -6 to 6
- rel_embed: float32 [201, 256], replicated, may hold values from -6 to 6
- weights: float32 [3, 256, 256], replicated, may hold values from -0.046875 to 0.046875
- cot: bfloat16 [65536, 256], P(('col', 'row')), may hold values from -6 to 6
- tile_row: int32 [16384], P(('row', 'col')), may hold values from 0 to 511, as said below
- tile_col: int32 [16384], P(('row', 'col')), may hold values from 0 to 511, as said below
- tile_live: int32 [256], P(('row', 'col')), may hold values from 1 to 64, as said below
- edge_ends: int32 [16384, 256], P(('row', 'col')), may hold values from 0 to 16383
- edge_relation: int32 [16384, 256], P(('row', 'col')), may hold values from 0 to 199
- edge_dir: int32 [16384, 256], P(('row', 'col')), may hold values 0 or 1
- edge_count: int32 [16384], P(('row', 'col')), may hold values from 1 to 256, as said below
Outputs:
- mixed: float32 [65536, 256], P(('col', 'row'))
- grad_feats: float32 [65536, 256], P(('row', 'col'))
- grad_rel: float32 [201, 256], replicated
- grad_weights: float32 [3, 256, 256], replicated
Inputs may be any that keep to these rules, and one draw needn't show every extreme that they name: `tile_row`: the slots of group k = i * 32 + j (j below 32) have block rows from j * 16 up to (j + 1) * 16 - 1. `tile_col`: the slots of group k = i * 32 + j have block columns from i * 64 up to (i + 1) * 64 - 1. `tile_live`: slots at or past the count are padding; some group is full in every draw. `edge_count`: edge slots at or past the count are padding; some tile slot is full in every draw.
All inputs are finite; a program needn't handle non-finite values. No bound on the sum of `edge_dir` on one device may be relied on, other than what follows from the above.
Results may differ from a plain program's by a relative error of at most 0.0003.
Values may be sent and summed in bfloat16 or wider, within the bound.
A program may use at most 128 MiB of HBM per device.

v0:
```python
import jax
import jax.numpy as jnp
from jax import lax
from jax.sharding import PartitionSpec as P

D = 256
TILE = 128
EDGE_TILE = 256


def product(left, right):
    return jnp.dot(left, right, precision=lax.Precision.HIGHEST, preferred_element_type=jnp.float32)


def shards(
    feats,
    rel_embed,
    weights,
    cot,
    tile_row,
    tile_col,
    tile_live,
    edge_ends,
    edge_relation,
    edge_dir,
    edge_count,
):
    rows_n = lax.axis_size("row")
    cols_n = lax.axis_size("col")
    row_index = lax.axis_index("row")
    col_index = lax.axis_index("col")
    ent_dev = feats.shape[0]
    src_dev = ent_dev * cols_n
    dst_dev = ent_dev * rows_n
    rels_all = rel_embed.shape[0]
    zero = jnp.int32(0)
    sources = lax.all_gather(feats, "col", axis=0, tiled=True)
    row_base = col_index * (dst_dev // TILE)
    column_start = row_index * (src_dev // TILE)
    live_tiles = tile_live[0]
    tile_iota = jnp.arange(TILE, dtype=jnp.int32)
    edge_iota = jnp.arange(EDGE_TILE, dtype=jnp.int32)
    rel_iota = jnp.arange(rels_all, dtype=jnp.int32)

    def tile_pieces(slot):
        ends = edge_ends[slot]
        valid = edge_iota < edge_count[slot]
        direction = edge_dir[slot]
        masks = jnp.stack([valid & (direction == 0), valid & (direction == 1)])
        onehot_dst = tile_iota[:, None] == (ends // TILE)[None, :]
        dst_split = (onehot_dst[None, :, :] & masks[:, None, :]).astype(jnp.bfloat16)
        onehot_src = ((ends % TILE)[:, None] == tile_iota[None, :]).astype(jnp.bfloat16)
        adjacency_tiles = jnp.einsum(
            "dve,eu->dvu", dst_split, onehot_src, preferred_element_type=jnp.float32
        ).astype(jnp.bfloat16)
        local_row = (tile_row[slot] - row_base) * TILE
        local_col = (tile_col[slot] - column_start) * TILE
        return (dst_split, adjacency_tiles, local_row, local_col)

    def forward_tile(slot, carry):
        totals, counts = carry
        dst_split, adjacency_tiles, local_row, local_col = tile_pieces(slot)
        onehot_rel = (rel_iota[:, None] == edge_relation[slot][None, :]).astype(jnp.bfloat16)
        block_entries = lax.dynamic_slice_in_dim(sources, local_col, TILE, 0)
        message_sum = jnp.einsum(
            "kzj,ji->kzi", adjacency_tiles, block_entries, preferred_element_type=jnp.float32
        )
        counted = jnp.einsum(
            "re,dve->drv", onehot_rel, dst_split, preferred_element_type=jnp.float32
        )
        totals = lax.dynamic_update_slice(
            totals,
            lax.dynamic_slice(totals, (zero, local_row, zero), (2, TILE, D)) + message_sum,
            (zero, local_row, zero),
        )
        counts = lax.dynamic_update_slice(
            counts,
            lax.dynamic_slice(counts, (zero, zero, local_row), (2, rels_all, TILE)) + counted,
            (zero, zero, local_row),
        )
        return (totals, counts)

    start = (
        jnp.zeros((2, dst_dev, D), jnp.float32),
        jnp.zeros((2, rels_all, dst_dev), jnp.float32),
    )
    totals, counts = lax.fori_loop(0, live_tiles, forward_tile, start)
    partial_value = totals - jnp.einsum(
        "gym,ye->gme",
        counts,
        rel_embed,
        precision=lax.Precision.HIGHEST,
        preferred_element_type=jnp.float32,
    )
    owner_flag = (row_index == col_index * rows_n // cols_n).astype(jnp.float32)
    offset = jnp.clip(col_index * dst_dev - row_index * src_dev, 0, src_dev - dst_dev)
    self_term = (
        lax.dynamic_slice_in_dim(sources, offset, dst_dev, 0).astype(jnp.float32)
        - rel_embed[rels_all - 1]
    ) * owner_flag
    stacked = jnp.concatenate([partial_value[0], partial_value[1], self_term], axis=1)
    owned = lax.psum_scatter(stacked, "row", scatter_dimension=0, tiled=True)
    own_in = owned[:, :D]
    own_out = owned[:, D : 2 * D]
    own_self = owned[:, 2 * D :]
    mixed = (
        product(own_in, weights[0]) + product(own_out, weights[1]) + product(own_self, weights[2])
    )
    cot_own = cot.astype(jnp.float32)
    local_images = jnp.stack([product(cot_own, weights[which].T) for which in range(3)])
    images = lax.all_gather(local_images, "row", axis=1, tiled=True)
    grad_local = jnp.stack(
        [product(own_in.T, cot_own), product(own_out.T, cot_own), product(own_self.T, cot_own)]
    )
    self_rel = -jnp.sum(local_images[2], axis=0)

    def backward_tile(slot, gathered):
        dst_split, adjacency_tiles, local_row, local_col = tile_pieces(slot)
        selected_rows = lax.dynamic_slice(images, (zero, local_row, zero), (2, TILE, D))
        scattered_messages = jnp.einsum(
            "tax,tam->xm",
            adjacency_tiles.astype(jnp.float32),
            selected_rows,
            precision=lax.Precision.HIGHEST,
            preferred_element_type=jnp.float32,
        )
        return lax.dynamic_update_slice_in_dim(
            gathered,
            lax.dynamic_slice_in_dim(gathered, local_col, TILE, 0) + scattered_messages,
            local_col,
            0,
        )

    gathered = lax.fori_loop(0, live_tiles, backward_tile, jnp.zeros((src_dev, D), jnp.float32))
    gathered = lax.dynamic_update_slice_in_dim(
        gathered,
        lax.dynamic_slice_in_dim(gathered, offset, dst_dev, 0) + images[2] * owner_flag,
        offset,
        0,
    )
    grad_feats = lax.psum_scatter(gathered, "col", scatter_dimension=0, tiled=True)
    rel_local = -jnp.einsum(
        "kha,kam->hm",
        counts,
        images[:2],
        precision=lax.Precision.HIGHEST,
        preferred_element_type=jnp.float32,
    )
    rel_local = rel_local.at[rels_all - 1].add(self_rel)
    grad_weights, grad_rel = lax.psum((grad_local, rel_local), ("row", "col"))
    return (mixed, grad_feats, grad_rel, grad_weights)


def solution(mesh):
    return jax.shard_map(
        shards,
        mesh=mesh,
        in_specs=(
            P(("row", "col"), None),
            P(),
            P(),
            P(("col", "row"), None),
            P(("row", "col")),
            P(("row", "col")),
            P(("row", "col")),
            P(("row", "col"), None),
            P(("row", "col"), None),
            P(("row", "col"), None),
            P(("row", "col")),
        ),
        out_specs=(P(("col", "row"), None), P(("row", "col"), None), P(), P()),
        check_vma=False,
    )
```

profile of v0, /device:TPU:6, one launch (start us, length us, event | category | flops | bytes accessed | tf_op | source)
XLA Modules:
  0.0 2299.3 jit_solution(5691225846461732551)
XLA Ops:
  13.9 53.9 %all-gather.3.cloned.1.call-done = bf16[8192,256]{0,1:T(8,128)(2,1)} async-done(((bf16[256,256]{0,1:T(8,128)(2,1)}), bf16[8192,256]{0,1:T(8,128)(2,1)}) %all-gather.3.cloned.1.call-update) | async-done | bytes 4194320 | tf_op jit(solution)/shard_map/all_gather | solution.py:37
  67.8 3.1 subtract_multiply_fusion
  70.9 2.5 broadcast_in_dim.6.clone
  73.8 778.5 %while.31 = (s32[]{:T(128)}, f32[2,2048,256]{1,2,0:T(8,128)}, f32[2,201,2048]{2,1,0:T(8,128)S(1)}, s32[]{:T(128)}, s32[64]{0:T(128)}, /*index=5*/s32[]{:T(128)},...) while((s32[]{:T(128)}, f32[2,2048,256]{1,2,0:T(8,128)}, ...), condition=%wide.region_1.2_spmd.clone.clone, body=%wide.region_0.1_spmd.clone.clone.sunk | while | flops 60306192 | bytes 3226499 | solution.py:87
  104.3 2.1 convolution_add_fusion.4
  122.8 2.1 convolution_add_fusion.4
  141.3 2.1 convolution_add_fusion.4
  197.0 2.1 convolution_add_fusion.4
  215.5 2.1 convolution_add_fusion.4
  234.0 2.1 convolution_add_fusion.4
  271.0 2.1 convolution_add_fusion.4
  326.6 2.1 convolution_add_fusion.4
  345.1 2.1 convolution_add_fusion.4
  363.7 2.1 convolution_add_fusion.4
  419.2 2.1 convolution_add_fusion.4
  437.8 2.1 convolution_add_fusion.4
  493.4 2.1 convolution_add_fusion.4
  548.9 2.1 convolution_add_fusion.4
  567.4 2.1 convolution_add_fusion.4
  585.9 2.1 convolution_add_fusion.4
  622.9 2.1 convolution_add_fusion.4
  641.5 2.1 convolution_add_fusion.4
  852.3 5.6 convolution_subtract_fusion
  859.5 3.0 pad_maximum_fusion
  862.6 7.3 fusion.51
  872.0 3.8 broadcast_in_dim.8
  875.7 422.7 %while.32 = (s32[]{:T(128)}, f32[8192,256]{1,0:T(8,128)}, s32[]{:T(128)}, s32[64]{0:T(128)}, s32[]{:T(128)}, /*index=5*/s32[64,256]{1,0:T(8,128)}, s32[64]{0:T(1...) while((s32[]{:T(128)}, f32[8192,256]{1,0:T(8,128)}, ...), condition=%wide.region_4.5_spmd.clone.clone, body=%wide.region_3.4_spmd.clone.clone.sunk | while | flops 117645576 | bytes 732011 | solution.py:134
  1298.4 44.1 %reduce-scatter.3.cloned.1.call-done = f32[256,768]{0,1:T(8,128)} async-done(((f32[2048,768]{0,1:T(8,128)}), f32[256,768]{0,1:T(8,128)}) %reduce-scatter.3.cloned.1.call-update) | async-done | bytes 786448 | tf_op jit(solution)/shard_map/reduce_scatter | solution.py:102
  1347.4 2.5 fusion.47
  1349.9 5.9 dynamic_update_slice.21
  1359.7 825.9 %all-reduce.3.cloned.1.call-done = (f32[201,256]{1,0:T(8,128)}, f32[3,256,256]{2,1,0:T(8,128)}) async-done(((f32[201,256]{1,0:T(8,128)}, f32[3,256,256]{2,1,0:T(8,128)}), (f32[201,256]{1,0:T(8,128)}, f32[3,256,256]{2,1,0:T(8,128)})) %all-reduce.3.cloned.1.call-update) | async-done | bytes 992272 | tf_op jit(solution)/shard_map/psum | solution.py:150
  2185.5 103.5 %reduce-scatter.5.cloned.1.call-done = f32[256,256]{1,0:T(8,128)} async-done(((f32[8192,256]{1,0:T(8,128)}), f32[256,256]{1,0:T(8,128)}) %reduce-scatter.5.cloned.1.call-update) | async-done | bytes 262160 | tf_op jit(solution)/shard_map/reduce_scatter | solution.py:141
  (1116 shorter events, 1016.0 us)
Async XLA Ops:
  7.2 1.8 copy-start
  7.2 60.6 %slice-start = ((f32[201,256]{1,0:T(8,128)}), f32[1,256]{1,0:T(1,128)S(1)}, s32[]{:S(2)}) async-start(f32[201,256]{1,0:T(8,128)} %param.18), calls=%async_computation.7 | async-start | bytes 2048 | tf_op jit(solution)/shard_map/slice | solution.py:99
  7.2 60.6 %all-gather.3.cloned.1.call-start = ((), (), s32[]{:S(2)}) async-start(), calls=%async_computation.2 | async-start | bytes 4325376 | tf_op jit(solution)/shard_map/all_gather | solution.py:37
  8.9 853.7 %all-gather.5.cloned.1.call-start = ((), (), s32[]{:S(2)}) async-start(), calls=%async_computation.4 | async-start | bytes 7077888 | tf_op jit(solution)/shard_map/all_gather | solution.py:111
  13.8 1328.7 %reduce-scatter.3.cloned.1.call-start = ((), (), s32[]{:S(2)}) async-start(), calls=%async_computation.3 | async-start | bytes 7077888 | tf_op jit(solution)/shard_map/reduce_scatter | solution.py:102
  857.9 1.6 copy-start.1
  862.5 1323.0 %all-reduce.3.cloned.1.call-start = ((), (), s32[]{:S(2)}) async-start(), calls=%async_computation.6 | async-start | bytes 1998848 | tf_op jit(solution)/shard_map/psum | solution.py:150
  870.0 0.7 copy-start.4
  1347.2 941.9 %reduce-scatter.5.cloned.1.call-start = ((), (), s32[]{:S(2)}) async-start(), calls=%async_computation.5 | async-start | bytes 8650752 | tf_op jit(solution)/shard_map/reduce_scatter | solution.py:141
  1355.8 1.1 copy-start.2
  1355.8 1.4 copy-start.3
Sparse Core Ops, SparseCore 0:
  11.1 56.6 all-gather.2
  70.2 74.5 all-gather.4
  862.7 479.8 reduce-scatter.2
  1348.5 836.9 all-reduce.2
  2190.5 98.4 reduce-scatter.4
where the time goes:
time: 2330 us; the launch traced here: 2300 us
  waiting for transfers between devices  1030 us (44%)
  local copies, waits for them, and re-layouts  627 us (27%)
  matrix products  245 us (11%)
  other arithmetic  215 us (9%)
  loops' own time  170 us (7%)
    psum x1, waiting for transfers between devices, shards(): grad_weights, grad_rel = lax.psum((grad_local, rel_local), ('row', 'col'))  826 us
    dynamic_update_slice x84, local copies, waits for them, and re-layouts, forward_tile(): lax.dynamic_update_slice(totals, lax.dynamic_slice(totals, (zero, local_r...  146 us
    dynamic_slice x84, local copies, waits for them, and re-layouts, forward_tile(): lax.dynamic_slice(totals, (zero, local_row, zero), (2, TILE, D))  145 us
    dynamic_slice x84, local copies, waits for them, and re-layouts, tile_pieces(): local_row = (tile_row[slot] - row_base) * TILE  104 us
    dynamic_slice x84, local copies, waits for them, and re-layouts, tile_pieces(): valid = edge_iota < edge_count[slot]  104 us
    dynamic_slice x84, local copies, waits for them, and re-layouts, tile_pieces(): local_col = (tile_col[slot] - column_start) * TILE  104 us
    reduce_scatter x1, waiting for transfers between devices, shards(): lax.psum_scatter(gathered, 'col', scatter_dimension=0, tiled=True)  104 us
    dot_general x42, matrix products, forward_tile(): jnp.einsum('kzj,ji->kzi', adjacency_tiles, block_entries, preferred_eleme...  89.1 us
  transfers between devices with their start and end apart: 5, of which 4 were waited for; matrix products, arithmetic and copies ran while one was open for 47% of the time, Pallas kernels for 0%

commit v1 on v0

v1 whole, which is shorter than its diff:
```python
import functools

import jax
import jax.numpy as jnp
from jax import lax
from jax.experimental import pallas as pl
from jax.experimental.pallas import tpu as pltpu
from jax.sharding import PartitionSpec as P

D = 256
TILE = 128
EDGE_TILE = 256
PAIR = 2 * TILE
RELS_PAD = 256
NONE = 1024
F32 = jnp.float32
BF16 = jnp.bfloat16
NN = (((1,), (0,)), ((), ()))
NT = (((1,), (1,)), ((), ()))
TN = (((0,), (0,)), ((), ()))


def dot(left, right, dims=NN):
    return lax.dot_general(left, right, dims, preferred_element_type=F32)


def split(value):
    high = value.astype(BF16)
    return high, (value - high.astype(F32)).astype(BF16)


def dot_exact_left(left, right, dims=NN):
    high, low = right
    return dot(left, high, dims) + dot(left, low, dims)


def dot_exact_right(left, right, dims=NN):
    high, low = left
    return dot(high, right, dims) + dot(low, right, dims)


def dot_split(left, right, dims=NN):
    return dot(left[0], right[0], dims) + (dot(left[0], right[1], dims) + dot(left[1], right[0], dims))


def rows_at(index, size):
    return pl.ds(pl.multiple_of(index * size, size), size)


def tiles_kernel(
    meta_ref,
    row_ref,
    col_ref,
    count_ref,
    ends_ref,
    relation_ref,
    dir_ref,
    feats_ref,
    cot_ref,
    rel_ref,
    weights_ref,
    grad_ref,
    mixed_ref,
    grad_weights_ref,
    grad_rel_ref,
    key_ref,
    src_ref,
    totals_ref,
    counts_ref,
    high_ref,
    low_ref,
):
    slots = ends_ref.shape[0]
    blocks = cot_ref.shape[0] // TILE
    rels_all = meta_ref[3]
    slot_iota = lax.broadcasted_iota(jnp.int32, (slots, EDGE_TILE), 0)
    edge_iota = lax.broadcasted_iota(jnp.int32, (slots, EDGE_TILE), 1)
    valid = (edge_iota < count_ref[...]) & (slot_iota < meta_ref[0])
    ends = ends_ref[...]
    key_ref[...] = jnp.where(valid, dir_ref[...] * TILE + lax.shift_right_logical(ends, 7), NONE)
    src_ref[...] = ends & (TILE - 1)

    weight = [split(weights_ref[which]) for which in range(3)]

    def image_block(block, _):
        cot = cot_ref[rows_at(block, TILE), :]
        pair = [dot_exact_left(cot, weight[which], NT) for which in range(2)]
        high, low = split(jnp.concatenate(pair, axis=0))
        at = rows_at(block, PAIR)
        high_ref[at, :] = high
        low_ref[at, :] = low
        totals_ref[at, :] = jnp.zeros((PAIR, D), F32)
        counts_ref[at, :] = jnp.zeros((PAIR, RELS_PAD), F32)
        return 0

    lax.fori_loop(0, blocks, image_block, 0)

    def clear_block(block, _):
        grad_ref[rows_at(block, PAIR), :] = jnp.zeros((PAIR, D), F32)
        return 0

    lax.fori_loop(0, grad_ref.shape[0] // PAIR, clear_block, 0)

    pair_iota = lax.broadcasted_iota(jnp.int32, (PAIR, EDGE_TILE), 0)
    tile_iota = lax.broadcasted_iota(jnp.int32, (TILE, EDGE_TILE), 0)

    def hot(iota, entries):
        return jnp.where(iota == entries, 1.0, 0.0).astype(BF16)

    def tile(slot, _):
        at = pl.ds(slot, 1)
        hot_dst = hot(pair_iota, key_ref[at, :])
        hot_src = hot(tile_iota, src_ref[at, :])
        hot_rel = hot(pair_iota, relation_ref[at, :])
        forward = dot(hot_dst, hot_src, NT).astype(BF16)
        backward = dot(hot_src, hot_dst, NT).astype(BF16)
        counted = dot(hot_dst, hot_rel, NT)
        row = rows_at(row_ref[slot], PAIR)
        col = rows_at(col_ref[slot], TILE)
        counts_ref[row, :] += counted
        totals_ref[row, :] += dot(forward, feats_ref[col, :])
        grad_ref[col, :] += dot(backward, high_ref[row, :]) + dot(backward, low_ref[row, :])
        return 0

    lax.fori_loop(0, slots, tile, 0, unroll=2)

    relations = split(rel_ref[...])
    grad_weights_ref[...] = jnp.zeros_like(grad_weights_ref)
    grad_rel_ref[...] = jnp.zeros_like(grad_rel_ref)

    def finish_block(block, _):
        at = rows_at(block, PAIR)
        counts = split(counts_ref[at, :])
        high, low = high_ref[at, :], low_ref[at, :]
        rel_part = dot(counts[0], high, TN) + (dot(counts[0], low, TN) + dot(counts[1], high, TN))
        grad_rel_ref[...] -= rel_part
        totals = totals_ref[at, :] - dot_split(counts, relations)
        total_in = split(totals[:TILE])
        total_out = split(totals[TILE:])
        here = rows_at(block, TILE)
        mixed_ref[here, :] = dot_split(total_in, weight[0]) + dot_split(total_out, weight[1])
        cot = cot_ref[here, :]
        grad_weights_ref[0] += dot_exact_right(total_in, cot, TN)
        grad_weights_ref[1] += dot_exact_right(total_out, cot, TN)
        return 0

    lax.fori_loop(0, blocks, finish_block, 0)

    @pl.when(meta_ref[1] == 1)
    def _():
        own_rel = rel_ref[pl.ds(rels_all - 1, 1), :]

        def self_block(block, total):
            here = rows_at(block, TILE)
            there = rows_at(meta_ref[2] + block, TILE)
            self_term = split(feats_ref[there, :].astype(F32) - own_rel)
            cot = cot_ref[here, :]
            mixed_ref[here, :] += dot_split(self_term, weight[2])
            grad_weights_ref[2] += dot_exact_right(self_term, cot, TN)
            image = dot_exact_left(cot, weight[2], NT)
            grad_ref[there, :] += image
            return total + jnp.sum(image, axis=0, keepdims=True)

        total = lax.fori_loop(0, blocks, self_block, jnp.zeros((1, D), F32))
        grad_rel_ref[pl.ds(rels_all - 1, 1), :] -= total


def tiles_call(meta, rows, cols, counts, ends, relation, direction, sources, cot, rel, weights):
    dst_dev, src_dev = cot.shape[0], sources.shape[0]
    slots = ends.shape[0]
    smem = pl.BlockSpec(memory_space=pltpu.SMEM)
    vmem = pl.BlockSpec(memory_space=pltpu.VMEM)
    return pl.pallas_call(
        tiles_kernel,
        out_shape=[
            jax.ShapeDtypeStruct((src_dev, D), F32),
            jax.ShapeDtypeStruct((dst_dev, D), F32),
            jax.ShapeDtypeStruct((3, D, D), F32),
            jax.ShapeDtypeStruct((RELS_PAD, D), F32),
        ],
        in_specs=[smem] * 3 + [vmem] * 8,
        out_specs=[vmem] * 4,
        scratch_shapes=[
            pltpu.VMEM((slots, EDGE_TILE), jnp.int32),
            pltpu.VMEM((slots, EDGE_TILE), jnp.int32),
            pltpu.VMEM((2 * dst_dev, D), F32),
            pltpu.VMEM((2 * dst_dev, RELS_PAD), F32),
            pltpu.VMEM((2 * dst_dev, D), BF16),
            pltpu.VMEM((2 * dst_dev, D), BF16),
        ],
        compiler_params=pltpu.CompilerParams(vmem_limit_bytes=56 * 1024 * 1024),
        name="tiles",
    )(meta, rows, cols, counts, ends, relation, direction, sources, cot, rel, weights)


def shards(
    feats,
    rel_embed,
    weights,
    cot,
    tile_row,
    tile_col,
    tile_live,
    edge_ends,
    edge_relation,
    edge_dir,
    edge_count,
):
    rows_n = lax.axis_size("row")
    cols_n = lax.axis_size("col")
    row_index = lax.axis_index("row")
    col_index = lax.axis_index("col")
    ent_dev = feats.shape[0]
    src_dev = ent_dev * cols_n
    dst_dev = ent_dev * rows_n
    rels_all = rel_embed.shape[0]
    sources = lax.all_gather(feats, "col", axis=0, tiled=True)
    targets = lax.all_gather(cot, "row", axis=0, tiled=True)
    owner = (row_index == col_index * rows_n // cols_n).astype(jnp.int32)
    offset = jnp.clip(col_index * dst_dev - row_index * src_dev, 0, src_dev - dst_dev) // TILE
    meta = jnp.stack([tile_live[0], owner, offset.astype(jnp.int32), jnp.int32(rels_all)])
    grad, mixed, grad_weights, grad_rel = tiles_call(
        meta,
        tile_row - col_index * (dst_dev // TILE),
        tile_col - row_index * (src_dev // TILE),
        edge_count[:, None],
        edge_ends,
        edge_relation,
        edge_dir,
        sources,
        targets,
        jnp.pad(rel_embed, ((0, RELS_PAD - rels_all), (0, 0))),
        weights,
    )
    grad_feats = lax.psum_scatter(grad, "col", scatter_dimension=0, tiled=True)
    mixed = lax.psum_scatter(mixed, "row", scatter_dimension=0, tiled=True)
    grad_weights, grad_rel = lax.psum((grad_weights, grad_rel[:rels_all]), ("row", "col"))
    return (mixed, grad_feats, grad_rel, grad_weights)


def solution(mesh):
    return jax.shard_map(
        shards,
        mesh=mesh,
        in_specs=(
            P(("row", "col"), None),
            P(),
            P(),
            P(("col", "row"), None),
            P(("row", "col")),
            P(("row", "col")),
            P(("row", "col")),
            P(("row", "col"), None),
            P(("row", "col"), None),
            P(("row", "col"), None),
            P(("row", "col")),
        ),
        out_specs=(P(("col", "row"), None), P(("row", "col"), None), P(), P()),
        check_vma=False,
    )
```

time: 2330 us -> 571 us (0.25); the launches traced: 2300 us -> 571 us
  local copies, waits for them, and re-layouts: 627 us -> 8.33 us
  waiting for transfers between devices: 1030 us -> 500 us
  matrix products: 245 us -> 0 us
  other arithmetic: 215 us -> 1.76 us
  loops' own time: 170 us -> 0 us
  Pallas kernels: 0 us -> 46.5 us
    psum x1, waiting for transfers between devices: 826 us -> 260 us  [shards(): lax.psum((grad_weights, grad_rel[:rels_all]), ('row', 'col'))]
    dynamic_slice x336 -> x0, local copies, waits for them, and re-layouts: 458 us -> none  [the longest x84 145 us: forward_tile(): lax.dynamic_slice(totals, (zero, local_row, zero), (2, TILE, D))]
    dot_general x179 -> x0, matrix products: 245 us -> none  [the longest x42 89.1 us: forward_tile(): jnp.einsum('kzj,ji->kzi', adjacency_tiles, block_entries, preferred_eleme...]
    another operation x2 -> x0, loops' own time: 170 us -> none  [the longest x1 85.2 us: shards(): lax.fori_loop(0, live_tiles, backward_tile, jnp.zeros((src_dev, D), jnp.f...]
    dynamic_update_slice x85 -> x0, local copies, waits for them, and re-layouts: 152 us -> none  [the longest x84 146 us: forward_tile(): lax.dynamic_update_slice(totals, lax.dynamic_slice(totals, (zero, local_r...]
    select_n x168 -> x0, other arithmetic: 61.5 us -> none  [the longest x84 60.8 us: tile_pieces(): onehot_dst = tile_iota[:, None] == (ends // TILE)[None, :]]
    and x84 -> x0, other arithmetic: 59.9 us -> none  [tile_pieces(): masks = jnp.stack([valid & (direction == 0), valid & (direction == 1)])]
    lt x84 -> x0, other arithmetic: 54.5 us -> none  [tile_pieces(): valid = edge_iota < edge_count[slot]]
  transfers between devices with their start and end apart: 5 -> 5, of which waited for: 4 -> 5; matrix products, arithmetic and copies ran while one was open for 47% -> 1% of each run, Pallas kernels for 0% -> 0%
where the time goes in v1:
time: 571 us
  waiting for transfers between devices  500 us (88%)
  Pallas kernels  46.5 us (8%)
  between operations  14.5 us (3%)
  local copies, waits for them, and re-layouts  8.33 us (1%)
    psum x1, waiting for transfers between devices, shards(): lax.psum((grad_weights, grad_rel[:rels_all]), ('row', 'col'))  260 us
    reduce_scatter x1, waiting for transfers between devices, shards(): grad_feats = lax.psum_scatter(grad, 'col', scatter_dimension=0, tiled=True)  104 us
    all_gather x1, waiting for transfers between devices, shards(): sources = lax.all_gather(feats, 'col', axis=0, tiled=True)  51.8 us
    pallas_call x1, Pallas kernels, tiles_call(): pl.pallas_call(tiles_kernel, out_shape=[jax.ShapeDtypeStruct((src_dev, D)...  46.5 us
    reduce_scatter x1, waiting for transfers between devices, shards(): mixed = lax.psum_scatter(mixed, 'row', scatter_dimension=0, tiled=True)  43.7 us
    all_gather x1, waiting for transfers between devices, shards(): targets = lax.all_gather(cot, 'row', axis=0, tiled=True)  37.3 us
  transfers between devices with their start and end apart: 5, of which 5 were waited for; matrix products, arithmetic and copies ran while one was open for 1% of the time, Pallas kernels for 0%

profile of v1, /device:TPU:6, one launch (start us, length us, event | category | flops | bytes accessed | tf_op | source)
XLA Modules:
  0.0 570.9 jit_solution(7711239202781471422)
XLA Ops:
  7.2 0.0 all-gather.5.cloned.1.call-start
  7.2 0.7 all-gather.5.cloned.1.call-update
  7.9 0.0 all-gather.3.cloned.1.call-start
  7.9 0.7 all-gather.3.cloned.1.call-update
  8.6 0.0 all-reduce.4.cloned.1.call-start
  9.4 1.4 copy.15.count_ref
  10.7 1.7 pad.4.rel_ref
  12.4 0.6 pad_add_fusion.meta_ref
  12.9 1.2 broadcast_subtract_fusion
  14.1 37.3 %all-gather.5.cloned.1.call-done.cot_ref = bf16[2048,256]{1,0:T(8,128)(2,1)} async-done(((bf16[256,256]{1,0:T(8,128)(2,1)}), bf16[2048,256]{1,0:T(8,128)(2,1)}) %all-gather.5.cloned.1.call-update) | async-done | bytes 1048592 | tf_op jit(solution)/shard_map/all_gather | solution.py:218
  51.4 51.8 %all-gather.3.cloned.1.call-done.feats_ref = bf16[8192,256]{1,0:T(8,128)(2,1)} async-done(((bf16[256,256]{1,0:T(8,128)(2,1)}), bf16[8192,256]{1,0:T(8,128)(2,1)}) %all-gather.3.cloned.1.call-update) | async-done | bytes 4194320 | tf_op jit(solution)/shard_map/all_gather | solution.py:217
  103.3 46.5 %tiles.1 = (f32[8192,256]{1,0:T(8,128)}, f32[2048,256]{1,0:T(8,128)}, f32[3,256,256]{2,1,0:T(8,128)}, f32[256,256]{1,0:T(8,128)}) custom-call(s32[4]{0:T(128)} %pad_add_fusion.meta_ref, s32[64]{0:T(128)} %get-tuple-element.15.row_ref, s32[64]{0:T(128)} %get-tuple-element.14.col_ref, s32[64,1]{1,0:T(8,128)} %copy.15.count_ref, s32[64,256]{1,0:T(8,128)} %ends_ref.1, ...), custom_call_target="tpu_custom_call" | custom-call | tf_op jit(solution)/shard_map/tiles/pallas_call | solution.py:173
  149.8 1.6 slice.3
  151.4 0.0 all-reduce.4.cloned.1.call-update
  151.4 0.0 reduce-scatter.3.cloned.1.call-start
  151.5 0.5 reduce-scatter.3.cloned.1.call-update
  152.0 0.0 reduce-scatter.5.cloned.1.call-start
  152.1 0.5 reduce-scatter.5.cloned.1.call-update
  152.6 260.4 %all-reduce.4.cloned.1.call-done = (f32[201,256]{1,0:T(8,128)}, f32[3,256,256]{2,1,0:T(8,128)}) async-done(((f32[201,256]{1,0:T(8,128)}, f32[3,256,256]{2,1,0:T(8,128)}), (f32[201,256]{1,0:T(8,128)}, f32[3,256,256]{2,1,0:T(8,128)})) %all-reduce.4.cloned.1.call-update) | async-done | bytes 992272 | tf_op jit(solution)/shard_map/psum | solution.py:237
  413.0 43.7 %reduce-scatter.3.cloned.1.call-done = f32[256,256]{1,0:T(8,128)} async-done(((f32[2048,256]{1,0:T(8,128)}), f32[256,256]{1,0:T(8,128)}) %reduce-scatter.3.cloned.1.call-update) | async-done | bytes 262160 | tf_op jit(solution)/shard_map/reduce_scatter | solution.py:236
  456.7 104.0 %reduce-scatter.5.cloned.1.call-done = f32[256,256]{1,0:T(8,128)} async-done(((f32[8192,256]{1,0:T(8,128)}), f32[256,256]{1,0:T(8,128)}) %reduce-scatter.5.cloned.1.call-update) | async-done | bytes 262160 | tf_op jit(solution)/shard_map/reduce_scatter | solution.py:235
  560.7 1.6 copy.19
  562.3 2.1 copy.20
Async XLA Ops:
  7.2 44.3 %all-gather.5.cloned.1.call-start = ((), (), s32[]{:S(2)}) async-start(), calls=%async_computation.3 | async-start | bytes 1179648 | tf_op jit(solution)/shard_map/all_gather | solution.py:218
  7.9 95.4 %all-gather.3.cloned.1.call-start = ((), (), s32[]{:S(2)}) async-start(), calls=%async_computation.2 | async-start | bytes 4325376 | tf_op jit(solution)/shard_map/all_gather | solution.py:217
  8.6 404.4 %all-reduce.4.cloned.1.call-start = ((), (), s32[]{:S(2)}) async-start(), calls=%async_computation.6 | async-start | bytes 1998848 | tf_op jit(solution)/shard_map/psum | solution.py:237
  151.4 305.3 %reduce-scatter.3.cloned.1.call-start = ((), (), s32[]{:S(2)}) async-start(), calls=%async_computation.4 | async-start | bytes 2359296 | tf_op jit(solution)/shard_map/reduce_scatter | solution.py:236
  152.0 408.7 %reduce-scatter.5.cloned.1.call-start = ((), (), s32[]{:S(2)}) async-start(), calls=%async_computation.5 | async-start | bytes 8650752 | tf_op jit(solution)/shard_map/reduce_scatter | solution.py:235
Sparse Core Ops, SparseCore 0:
  9.8 41.6 all-gather.4
  54.0 49.2 all-gather.2
  151.6 261.4 all-reduce.3
  416.2 40.4 reduce-scatter.2
  461.7 98.9 reduce-scatter.4

commit v2 on v1

--- a/solution.py
+++ b/solution.py
@@ -61,8 +61,7 @@
     weights_ref,
     grad_ref,
     mixed_ref,
-    grad_weights_ref,
-    grad_rel_ref,
+    sums_ref,
     key_ref,
     src_ref,
     totals_ref,
@@ -125,23 +124,24 @@
     lax.fori_loop(0, slots, tile, 0, unroll=2)
 
     relations = split(rel_ref[...])
-    grad_weights_ref[...] = jnp.zeros_like(grad_weights_ref)
-    grad_rel_ref[...] = jnp.zeros_like(grad_rel_ref)
+    sums_ref[...] = jnp.zeros_like(sums_ref)
+    weights_at = [pl.ds(which * D, D) for which in range(3)]
+    rel_at = pl.ds(3 * D, RELS_PAD)
 
     def finish_block(block, _):
         at = rows_at(block, PAIR)
         counts = split(counts_ref[at, :])
         high, low = high_ref[at, :], low_ref[at, :]
         rel_part = dot(counts[0], high, TN) + (dot(counts[0], low, TN) + dot(counts[1], high, TN))
-        grad_rel_ref[...] -= rel_part
+        sums_ref[rel_at, :] -= rel_part
         totals = totals_ref[at, :] - dot_split(counts, relations)
         total_in = split(totals[:TILE])
         total_out = split(totals[TILE:])
         here = rows_at(block, TILE)
         mixed_ref[here, :] = dot_split(total_in, weight[0]) + dot_split(total_out, weight[1])
         cot = cot_ref[here, :]
-        grad_weights_ref[0] += dot_exact_right(total_in, cot, TN)
-        grad_weights_ref[1] += dot_exact_right(total_out, cot, TN)
+        sums_ref[weights_at[0], :] += dot_exact_right(total_in, cot, TN)
+        sums_ref[weights_at[1], :] += dot_exact_right(total_out, cot, TN)
         return 0
 
     lax.fori_loop(0, blocks, finish_block, 0)
@@ -156,13 +156,13 @@
             self_term = split(feats_ref[there, :].astype(F32) - own_rel)
             cot = cot_ref[here, :]
             mixed_ref[here, :] += dot_split(self_term, weight[2])
-            grad_weights_ref[2] += dot_exact_right(self_term, cot, TN)
+            sums_ref[weights_at[2], :] += dot_exact_right(self_term, cot, TN)
             image = dot_exact_left(cot, weight[2], NT)
             grad_ref[there, :] += image
             return total + jnp.sum(image, axis=0, keepdims=True)
 
         total = lax.fori_loop(0, blocks, self_block, jnp.zeros((1, D), F32))
-        grad_rel_ref[pl.ds(rels_all - 1, 1), :] -= total
+        sums_ref[pl.ds(3 * D + rels_all - 1, 1), :] -= total
 
 
 def tiles_call(meta, rows, cols, counts, ends, relation, direction, sources, cot, rel, weights):
@@ -175,11 +175,10 @@
         out_shape=[
             jax.ShapeDtypeStruct((src_dev, D), F32),
             jax.ShapeDtypeStruct((dst_dev, D), F32),
-            jax.ShapeDtypeStruct((3, D, D), F32),
-            jax.ShapeDtypeStruct((RELS_PAD, D), F32),
+            jax.ShapeDtypeStruct((3 * D + RELS_PAD, D), F32),
         ],
         in_specs=[smem] * 3 + [vmem] * 8,
-        out_specs=[vmem] * 4,
+        out_specs=[vmem] * 3,
         scratch_shapes=[
             pltpu.VMEM((slots, EDGE_TILE), jnp.int32),
             pltpu.VMEM((slots, EDGE_TILE), jnp.int32),
@@ -191,6 +190,476 @@
         compiler_params=pltpu.CompilerParams(vmem_limit_bytes=56 * 1024 * 1024),
         name="tiles",
     )(meta, rows, cols, counts, ends, relation, direction, sources, cot, rel, weights)
+
+
+MESH = pl.DeviceIdType.MESH
+RING = 4
+HALF = TILE
+
+
+class Copies:
+    def __init__(self, send_sems):
+        self.send_sems, self.started = send_sems, []
+
+    def start(self, src, dst, recv, peer):
+        copy = pltpu.make_async_remote_copy(
+            src_ref=src,
+            dst_ref=dst,
+            send_sem=self.send_sems.at[len(self.started)],
+            recv_sem=recv,
+            device_id=peer,
+            device_id_type=MESH,
+        )
+        copy.start()
+        self.started.append(copy)
+
+    def received(self, dst, recv):
+        pltpu.make_async_remote_copy(
+            src_ref=dst,
+            dst_ref=dst,
+            send_sem=self.send_sems.at[0],
+            recv_sem=recv,
+            device_id=self.any_peer,
+            device_id_type=MESH,
+        ).wait_recv()
+
+    def finish(self):
+        for copy in self.started:
+            copy.wait_send()
+
+
+class Place:
+    def __init__(self):
+        self.row = lax.axis_index("row")
+        self.col = lax.axis_index("col")
+        self.core = self.col % 2
+        self.stride1 = 8 - 6 * self.core
+        self.stride2 = 10 - self.stride1
+        self.p1 = self.col // self.stride1 % RING
+        self.p2 = self.col // self.stride2 % RING
+
+    def col_at(self, k1, k2):
+        return (self.p1 + k1) % RING * self.stride1 + (self.p2 + k2) % RING * self.stride2 + self.core
+
+    def peer(self, k1, k2):
+        return (self.row, self.col_at(k1, k2))
+
+    def partner(self):
+        return (self.row, self.col + 1 - 2 * self.core)
+
+    def along_row(self, k, rows):
+        return ((self.row + k) % rows, self.col)
+
+    def greet(self, peers):
+        barrier = pltpu.get_barrier_semaphore()
+        for peer in peers:
+            pl.semaphore_signal(barrier, inc=1, device_id=peer, device_id_type=MESH)
+        pl.semaphore_wait(barrier, len(peers))
+
+
+def run_in_order(pipes, order):
+    for name in order:
+        next(pipes[name], None)
+    for pipe in pipes.values():
+        for _ in pipe:
+            pass
+
+
+def gather_kernel(rows, feats_ref, cot_ref, sources_ref, targets_ref, send_sems, shard_sems, row_sems, own_sems):
+    place = Place()
+    copies = Copies(send_sems)
+    copies.any_peer = place.partner()
+    own_copies = [
+        pltpu.make_async_copy(feats_ref, sources_ref.at[place.col], own_sems.at[0]),
+        pltpu.make_async_copy(cot_ref, targets_ref.at[place.row], own_sems.at[1]),
+    ]
+    for copy in own_copies:
+        copy.start()
+    place.greet(
+        [place.partner()]
+        + [place.peer(k, 0) for k in (1, 3)]
+        + [place.peer(0, k) for k in (1, 3)]
+        + [place.along_row(k, rows) for k in (1, rows - 1)]
+    )
+    parts = [pl.ds(0, HALF), pl.ds(HALF, HALF)]
+
+    def send_shard(b, which, peer, src=None):
+        for half in which:
+            here = sources_ref.at[b, parts[half]]
+            copies.start(here if src is None else src.at[parts[half]], here, shard_sems.at[2 * b + half], peer)
+
+    def got_shard(b, which):
+        for half in which:
+            copies.received(sources_ref.at[b, parts[half]], shard_sems.at[2 * b + half])
+
+    def feats_pipe():
+        for half in (0, 1):
+            for peer in (place.peer(1, 0), place.peer(3, 0)):
+                send_shard(place.col, [half], peer, feats_ref)
+        for peer in (place.peer(0, 1), place.peer(0, 3), place.partner()):
+            send_shard(place.col, [0, 1], peer, feats_ref)
+        yield
+
+        def spread(b, which):
+            for peer in (place.peer(0, 1), place.peer(0, 3)):
+                send_shard(b, which, peer)
+            send_shard(b, which, place.partner())
+
+        left, right, far = place.col_at(3, 0), place.col_at(1, 0), place.col_at(2, 0)
+        got_shard(left, [0])
+        send_shard(left, [0], place.peer(1, 0))
+        spread(left, [0])
+        got_shard(right, [0])
+        spread(right, [0])
+        got_shard(right, [1])
+        send_shard(right, [1], place.peer(3, 0))
+        spread(right, [1])
+        got_shard(left, [1])
+        spread(left, [1])
+        yield
+
+        def second(k1):
+            below, above = place.col_at(k1, 3), place.col_at(k1, 1)
+            got_shard(below, [0])
+            send_shard(below, [0], place.peer(0, 1))
+            got_shard(above, [0])
+            got_shard(above, [1])
+            send_shard(above, [1], place.peer(0, 3))
+            got_shard(below, [1])
+            send_shard(below, [0, 1], place.partner())
+            send_shard(above, [0, 1], place.partner())
+
+        second(0)
+        yield
+        got_shard(far, [0, 1])
+        spread(far, [0, 1])
+        yield
+        second(3)
+        yield
+        second(1)
+        yield
+        second(2)
+        yield
+        for k1 in (0, 3, 1, 2):
+            b = place.col_at(k1, 2)
+            got_shard(b, [0, 1])
+            send_shard(b, [0, 1], place.partner())
+        yield
+        for k1 in range(RING):
+            for k2 in range(RING):
+                got_shard(place.col_at(k1, k2) + 1 - 2 * place.core, [0, 1])
+
+    def cot_pipe():
+        after, before = place.along_row(1, rows), place.along_row(rows - 1, rows)
+
+        def send_row(index, which, peer, src=None):
+            for half in which:
+                here = targets_ref.at[index, parts[half]]
+                copies.start(here if src is None else src.at[parts[half]], here, row_sems.at[2 * index + half], peer)
+
+        def got_row(index, which):
+            for half in which:
+                copies.received(targets_ref.at[index, parts[half]], row_sems.at[2 * index + half])
+
+        send_row(place.row, [0, 1], after, cot_ref)
+        send_row(place.row, [1, 0], before, cot_ref)
+        yield
+        for k in range(1, rows // 2):
+            last = k == rows // 2 - 1
+            low, high = (place.row + rows - k) % rows, (place.row + k) % rows
+            got_row(low, [0])
+            send_row(low, [0], after)
+            got_row(high, [1])
+            send_row(high, [1], before)
+            got_row(low, [1])
+            if not last:
+                send_row(low, [1], after)
+            got_row(high, [0])
+            if not last:
+                send_row(high, [0], before)
+            yield
+        got_row((place.row + rows // 2) % rows, [0, 1])
+
+    run_in_order({"f": feats_pipe(), "c": cot_pipe()}, "fcfcffcffcff")
+    for copy in own_copies:
+        copy.wait()
+    copies.finish()
+
+
+def gather_call(feats, cot, rows, cols):
+    anywhere = pl.BlockSpec(memory_space=pl.ANY)
+    vmem = pl.BlockSpec(memory_space=pltpu.VMEM)
+    sources, targets = pl.pallas_call(
+        functools.partial(gather_kernel, rows),
+        out_shape=[
+            jax.ShapeDtypeStruct((cols,) + feats.shape, feats.dtype),
+            jax.ShapeDtypeStruct((rows,) + cot.shape, cot.dtype),
+        ],
+        in_specs=[vmem, vmem],
+        out_specs=[anywhere, anywhere],
+        scratch_shapes=[
+            pltpu.SemaphoreType.DMA((160,)),
+            pltpu.SemaphoreType.DMA((2 * cols,)),
+            pltpu.SemaphoreType.DMA((2 * rows,)),
+            pltpu.SemaphoreType.DMA((2,)),
+        ],
+        compiler_params=pltpu.CompilerParams(
+            collective_id=0, has_side_effects=True, vmem_limit_bytes=32 * 1024 * 1024
+        ),
+        name="gather",
+    )(feats, cot)
+    return sources.reshape(-1, D), targets.reshape(-1, D)
+
+
+def reduce_kernel(
+    rows,
+    grad_any,
+    mixed_in,
+    sums_in,
+    grad_out,
+    mixed_out,
+    sums_out,
+    grad_acc,
+    pair_in,
+    relay1,
+    ring1,
+    relay2,
+    ring2,
+    row_up,
+    row_down,
+    sum_pair,
+    sum_first,
+    sum_second,
+    sum_rows,
+    sum_tiles,
+    send_sems,
+    own_sems,
+    pair_sems,
+    ring_sems,
+    row_sems,
+    sum_sems,
+    spread_sems,
+):
+    place = Place()
+    copies = Copies(send_sems)
+    copies.any_peer = place.partner()
+    partner = place.partner()
+    core = place.core
+    order1 = (2, 1, 3, 0)
+    own_copies = {}
+    for k in order1:
+        for r in (2, 1, 3, 0):
+            block = place.col_at(k, r) // 2
+            copy = pltpu.make_async_copy(grad_any.at[block, core], grad_acc.at[k, r], own_sems.at[4 * k + r])
+            copy.start()
+            own_copies[k, r] = copy
+    place.greet(
+        [partner]
+        + [place.peer(k1, k2) for k1 in range(RING) for k2 in range(RING) if k1 or k2]
+        + [place.along_row(k, rows) for k in range(1, rows)]
+    )
+    low, high = pl.ds(0, HALF), pl.ds(HALF, HALF)
+
+    def grad_pipe():
+        for k in order1:
+            for r in (2, 1, 3, 0):
+                block = ((place.p2 + k) % RING * place.stride2 + (place.p1 + r) % RING * place.stride1) // 2
+                copies.start(grad_any.at[block, 1 - core], pair_in.at[k, r], pair_sems.at[4 * k + r], partner)
+        yield
+
+        def pair_sum(k, r):
+            own_copies[k, r].wait()
+            copies.received(pair_in.at[k, r], pair_sems.at[4 * k + r])
+            grad_acc[k, r] += pair_in[k, r]
+
+        right, left = place.peer(1, 0), place.peer(3, 0)
+        for r in range(RING):
+            pair_sum(2, r)
+        copies.start(grad_acc.at[2, pl.ds(0, 2)], relay1.at[0], ring_sems.at[0], right)
+        copies.start(grad_acc.at[2, pl.ds(2, 2)], relay1.at[1], ring_sems.at[1], left)
+        yield
+        for r in (2, 3):
+            pair_sum(1, r)
+        copies.start(grad_acc.at[1, pl.ds(2, 2)], ring1.at[0, pl.ds(2, 2)], ring_sems.at[3], right)
+        for r in (0, 1):
+            pair_sum(3, r)
+        copies.start(grad_acc.at[3, pl.ds(0, 2)], ring1.at[1, pl.ds(0, 2)], ring_sems.at[4], left)
+        yield
+        for r in (0, 1):
+            pair_sum(1, r)
+        for r in (2, 3):
+            pair_sum(3, r)
+        for r in range(RING):
+            pair_sum(0, r)
+        yield
+        copies.received(relay1.at[0], ring_sems.at[0])
+        for r in (0, 1):
+            grad_acc[1, r] += relay1[0, r]
+        copies.start(grad_acc.at[1, pl.ds(0, 2)], ring1.at[0, pl.ds(0, 2)], ring_sems.at[2], right)
+        copies.received(relay1.at[1], ring_sems.at[1])
+        for r in (0, 1):
+            grad_acc[3, 2 + r] += relay1[1, r]
+        copies.start(grad_acc.at[3, pl.ds(2, 2)], ring1.at[1, pl.ds(2, 2)], ring_sems.at[5], left)
+        yield
+        copies.received(ring1.at[0, pl.ds(2, 2)], ring_sems.at[3])
+        copies.received(ring1.at[1, pl.ds(0, 2)], ring_sems.at[4])
+        for r in (2, 3):
+            grad_acc[0, r] += ring1[0, r]
+        for r in (0, 1):
+            grad_acc[0, r] += ring1[1, r]
+        yield
+        up, down = place.peer(0, 1), place.peer(0, 3)
+        copies.received(ring1.at[1, pl.ds(2, 2)], ring_sems.at[5])
+        grad_acc[0, 2] += ring1[1, 2]
+        copies.start(grad_acc.at[0, 2, low], relay2.at[0], ring_sems.at[6], up)
+        copies.start(grad_acc.at[0, 2, high], relay2.at[1], ring_sems.at[7], down)
+        grad_acc[0, 3] += ring1[1, 3]
+        copies.start(grad_acc.at[0, 3, low], ring2.at[1, low], ring_sems.at[10], down)
+        copies.received(ring1.at[0, pl.ds(0, 2)], ring_sems.at[2])
+        grad_acc[0, 1] += ring1[0, 1]
+        copies.start(grad_acc.at[0, 1, high], ring2.at[0, high], ring_sems.at[9], up)
+        grad_acc[0, 0] += ring1[0, 0]
+        yield
+        copies.received(relay2.at[0], ring_sems.at[6])
+        grad_acc[0, 1, low] += relay2[0]
+        copies.start(grad_acc.at[0, 1, low], ring2.at[0, low], ring_sems.at[8], up)
+        copies.received(relay2.at[1], ring_sems.at[7])
+        grad_acc[0, 3, high] += relay2[1]
+        copies.start(grad_acc.at[0, 3, high], ring2.at[1, high], ring_sems.at[11], down)
+        yield
+        copies.received(ring2.at[0, high], ring_sems.at[9])
+        copies.received(ring2.at[1, low], ring_sems.at[10])
+        copies.received(ring2.at[0, low], ring_sems.at[8])
+        copies.received(ring2.at[1, high], ring_sems.at[11])
+        grad_out[...] = grad_acc[0, 0] + ring2[0] + ring2[1]
+
+    def mixed_pipe():
+        after, before = place.along_row(1, rows), place.along_row(rows - 1, rows)
+        copies.start(mixed_in.at[(place.row + rows - 1) % rows, low], row_up.at[0], row_sems.at[0], after)
+        copies.start(mixed_in.at[(place.row + 1) % rows, high], row_down.at[0], row_sems.at[rows], before)
+        yield
+        for step in range(1, rows):
+            copies.received(row_up.at[step - 1], row_sems.at[step - 1])
+            row_up[step - 1] += mixed_in[(place.row + 2 * rows - 1 - step) % rows, low]
+            if step < rows - 1:
+                copies.start(row_up.at[step - 1], row_up.at[step], row_sems.at[step], after)
+            copies.received(row_down.at[step - 1], row_sems.at[rows + step - 1])
+            row_down[step - 1] += mixed_in[(place.row + 1 + step) % rows, high]
+            if step < rows - 1:
+                copies.start(row_down.at[step - 1], row_down.at[step], row_sems.at[rows + step], before)
+            yield
+        mixed_out[low] = row_up[rows - 2]
+        mixed_out[high] = row_down[rows - 2]
+
+    def sums_pipe():
+        copies.start(sums_in.at[1 - core], sum_pair, sum_sems.at[0], partner)
+        yield
+        copies.received(sum_pair, sum_sems.at[0])
+        for q in range(RING):
+            sum_pair[q] += sums_in[core, q]
+        for k in (2, 1, 3):
+            copies.start(sum_pair.at[(place.p1 + k) % RING], sum_first.at[k], sum_sems.at[k], place.peer(k, 0))
+        sum_first[0] = sum_pair[place.p1]
+        yield
+        for k in (1, 3, 2):
+            copies.received(sum_first.at[k], sum_sems.at[k])
+            sum_first[0] += sum_first[k]
+        for k in (2, 1, 3):
+            copies.start(sum_first.at[0, (place.p2 + k) % RING], sum_second.at[k], sum_sems.at[3 + k], place.peer(0, k))
+        sum_second[0] = sum_first[0, place.p2]
+        yield
+        for k in (1, 3, 2):
+            copies.received(sum_second.at[k], sum_sems.at[3 + k])
+            sum_second[0] += sum_second[k]
+        for quarter in range(RING):
+            for side in range(2):
+                sum_tiles[2 * quarter + side] = sum_second[0, pl.ds(8 * quarter, 8), pl.ds(TILE * side, TILE)]
+        for k in (4, 3, 5, 2, 6, 1, 7):
+            copies.start(
+                sum_tiles.at[(place.row + k) % rows], sum_rows.at[k], sum_sems.at[6 + k], place.along_row(k, rows)
+            )
+        sum_rows[0] = sum_tiles[place.row]
+        yield
+        for k in (1, 7, 2, 6, 3, 5, 4):
+            copies.received(sum_rows.at[k], sum_sems.at[6 + k])
+            sum_rows[0] += sum_rows[k]
+        for k in (4, 3, 5, 2, 6, 1, 7):
+            copies.start(
+                sum_rows.at[0], sum_tiles.at[rows + place.row], sum_sems.at[13 + k], place.along_row(k, rows)
+            )
+        sum_tiles[rows + place.row] = sum_rows[0]
+        yield
+        for k in (1, 7, 2, 6, 3, 5, 4):
+            copies.received(sum_tiles.at[rows + (place.row + rows - k) % rows], sum_sems.at[13 + k])
+        own = sums_out.at[core, place.p1, place.p2]
+        for quarter in range(RING):
+            for side in range(2):
+                own[pl.ds(8 * quarter, 8), pl.ds(TILE * side, TILE)] = sum_tiles[rows + 2 * quarter + side]
+        others = [(k1, k2) for k1 in range(RING) for k2 in range(RING) if k1 or k2]
+        for k1, k2 in others:
+            copies.start(own, own, spread_sems.at[4 * k1 + k2], place.peer(k1, k2))
+        yield
+        for k1, k2 in others:
+            there = sums_out.at[core, (place.p1 + RING - k1) % RING, (place.p2 + RING - k2) % RING]
+            copies.received(there, spread_sems.at[4 * k1 + k2])
+        copies.start(sums_out.at[core], sums_out.at[core], spread_sems.at[0], partner)
+        yield
+        copies.received(sums_out.at[1 - core], spread_sems.at[0])
+
+    run_in_order(
+        {"s": sums_pipe(), "m": mixed_pipe(), "g": grad_pipe()},
+        "smg" + "s" + "g" + "m" + "s" + "g" + "m" + "s" + "g" + "s" + "m" + "g" + "s" + "m" + "g" + "m" + "s" + "g" + "m" + "g" + "m" + "s" + "g",
+    )
+    copies.finish()
+
+
+def reduce_call(grad, mixed, sums, rows, cols):
+    anywhere = pl.BlockSpec(memory_space=pl.ANY)
+    vmem = pl.BlockSpec(memory_space=pltpu.VMEM)
+    ent_dev = grad.shape[0] // cols
+    block = (ent_dev, D)
+    share = sums.shape[0] // cols
+    grad_out, mixed_out, sums_out = pl.pallas_call(
+        functools.partial(reduce_kernel, rows),
+        out_shape=[
+            jax.ShapeDtypeStruct(block, F32),
+            jax.ShapeDtypeStruct(block, F32),
+            jax.ShapeDtypeStruct((2, RING, RING, share, D), F32),
+        ],
+        in_specs=[anywhere, vmem, vmem],
+        out_specs=[vmem] * 3,
+        scratch_shapes=[
+            pltpu.VMEM((RING, RING) + block, F32),
+            pltpu.VMEM((RING, RING) + block, F32),
+            pltpu.VMEM((2, 2) + block, F32),
+            pltpu.VMEM((2, RING) + block, F32),
+            pltpu.VMEM((2, HALF, D), F32),
+            pltpu.VMEM((2,) + block, F32),
+            pltpu.VMEM((rows - 1, HALF, D), F32),
+            pltpu.VMEM((rows - 1, HALF, D), F32),
+            pltpu.VMEM((RING, RING, share, D), F32),
+            pltpu.VMEM((RING, RING, share, D), F32),
+            pltpu.VMEM((RING, share, D), F32),
+            pltpu.VMEM((rows, 8, TILE), F32),
+            pltpu.VMEM((2 * rows, 8, TILE), F32),
+            pltpu.SemaphoreType.DMA((96,)),
+            pltpu.SemaphoreType.DMA((16,)),
+            pltpu.SemaphoreType.DMA((16,)),
+            pltpu.SemaphoreType.DMA((12,)),
+            pltpu.SemaphoreType.DMA((2 * rows,)),
+            pltpu.SemaphoreType.DMA((24,)),
+            pltpu.SemaphoreType.DMA((16,)),
+        ],
+        compiler_params=pltpu.CompilerParams(
+            collective_id=1, has_side_effects=True, vmem_limit_bytes=48 * 1024 * 1024
+        ),
+        name="reduce",
+    )(
+        grad.reshape((cols // 2, 2) + block),
+        mixed.reshape((rows,) + block),
+        sums.reshape(2, RING, RING, share, D),
+    )
+    return grad_out, mixed_out, sums_out.reshape(-1, D)
 
 
 def shards(
@@ -214,12 +683,11 @@
     src_dev = ent_dev * cols_n
     dst_dev = ent_dev * rows_n
     rels_all = rel_embed.shape[0]
-    sources = lax.all_gather(feats, "col", axis=0, tiled=True)
-    targets = lax.all_gather(cot, "row", axis=0, tiled=True)
+    sources, targets = gather_call(feats, cot, rows_n, cols_n)
     owner = (row_index == col_index * rows_n // cols_n).astype(jnp.int32)
     offset = jnp.clip(col_index * dst_dev - row_index * src_dev, 0, src_dev - dst_dev) // TILE
     meta = jnp.stack([tile_live[0], owner, offset.astype(jnp.int32), jnp.int32(rels_all)])
-    grad, mixed, grad_weights, grad_rel = tiles_call(
+    grad, mixed, sums = tiles_call(
         meta,
         tile_row - col_index * (dst_dev // TILE),
         tile_col - row_index * (src_dev // TILE),
@@ -232,10 +700,9 @@
         jnp.pad(rel_embed, ((0, RELS_PAD - rels_all), (0, 0))),
         weights,
     )
-    grad_feats = lax.psum_scatter(grad, "col", scatter_dimension=0, tiled=True)
-    mixed = lax.psum_scatter(mixed, "row", scatter_dimension=0, tiled=True)
-    grad_weights, grad_rel = lax.psum((grad_weights, grad_rel[:rels_all]), ("row", "col"))
-    return (mixed, grad_feats, grad_rel, grad_weights)
+    grad_feats, mixed, sums = reduce_call(grad, mixed, sums, rows_n, cols_n)
+    grad_rel = sums[3 * D : 3 * D + rels_all]
+    return (mixed, grad_feats, grad_rel, sums[: 3 * D].reshape(3, D, D))
 
 
 def solution(mesh):

time: 571 us -> 145 us (0.25)
  waiting for transfers between devices: 500 us -> 0 us
  Pallas kernels: 46.5 us -> 125 us
  between operations: 14.5 us -> 1.34 us
    psum x1 -> x0, waiting for transfers between devices: 260 us -> none  [shards(): lax.psum((grad_weights, grad_rel[:rels_all]), ('row', 'col'))]
    reduce_scatter x2 -> x0, waiting for transfers between devices: 148 us -> none  [the longest x1 104 us: shards(): grad_feats = lax.psum_scatter(grad, 'col', scatter_dimension=0, tiled=True)]
    all_gather x2 -> x0, waiting for transfers between devices: 89.1 us -> none  [the longest x1 51.8 us: shards(): sources = lax.all_gather(feats, 'col', axis=0, tiled=True)]
    pallas_call x0 -> x2, Pallas kernels: none -> 78.9 us  [the longest x1 50.2 us: reduce_call(): pl.pallas_call(functools.partial(reduce_kernel, rows), out_shape=[jax.Sha...]
  transfers between devices with their start and end apart: 5 -> 0, of which waited for: 5 -> 0; matrix products, arithmetic and copies ran while one was open for 1% -> 0% of each run, Pallas kernels for 0% -> 0%
where the time goes in v2:
time: 145 us; the launch traced here: 142 us
  Pallas kernels  125 us (86%)
  local copies, waits for them, and re-layouts  13.6 us (9%)
  other arithmetic  1.79 us (1%)
    pallas_call x1, Pallas kernels, reduce_call(): pl.pallas_call(functools.partial(reduce_kernel, rows), out_shape=[jax.Sha...  50.2 us
    pallas_call x1, Pallas kernels, tiles_call(): pl.pallas_call(tiles_kernel, out_shape=[jax.ShapeDtypeStruct((src_dev, D)...  46.3 us
    pallas_call x1, Pallas kernels, gather_call(): pl.pallas_call(functools.partial(gather_kernel, rows), out_shape=[jax.Sha...  28.7 us
    unnamed x14, local copies, waits for them, and re-layouts  8.97 us

profile of v2, /device:TPU:6, one launch (start us, length us, event | category | flops | bytes accessed | tf_op | source)
XLA Modules:
  0.0 141.9 jit_solution(2776220065333070530)
XLA Ops:
  1.3 0.6 pad_add_fusion.meta_ref
  1.9 1.2 broadcast_subtract_fusion
  3.1 1.4 copy.15.count_ref
  4.5 1.7 %pad.4.rel_ref = f32[256,256]{1,0:T(8,128)} pad(f32[201,256]{1,0:T(8,128)} %param.12, f32[]{:T(128)} %constant.54.clone.1), padding=0_55x0_0 | pad | bytes 467972 | tf_op jit(solution)/shard_map/jit(_pad)/pad | solution.py:700
  6.1 0.0 copy-start.4
  6.1 0.9 copy-done.4
  7.0 0.0 copy-start.5
  7.0 0.9 copy-done.5
  7.9 28.7 %gather.1 = (bf16[32,256,256]{2,1,0:T(8,128)(2,1)S(1)}, bf16[8,256,256]{2,1,0:T(8,128)(2,1)S(1)}) custom-call(bf16[256,256]{1,0:T(8,128)(2,1)S(1)} %copy-done.4, bf16[256,256]{1,0:T(8,128)(2,1)S(1)} %copy-done.5), custom_call_target="tpu_custom_call" | custom-call | tf_op jit(solution)/shard_map/gather/pallas_call | solution.py:392
  36.6 0.0 copy-start
  36.6 2.0 %copy-done = bf16[32,256,256]{2,1,0:T(8,128)(2,1)} copy-done((bf16[32,256,256]{2,1,0:T(8,128)(2,1)}, bf16[32,256,256]{2,1,0:T(8,128)(2,1)S(1)}, u32[]{:S(2)}) %copy-start) | copy-done | bytes 4194328
  38.6 0.0 copy-start.2
  38.6 1.0 copy-done.2
  39.5 46.3 %tiles.1 = (f32[8192,256]{1,0:T(8,128)}, f32[2048,256]{1,0:T(8,128)}, f32[1024,256]{1,0:T(8,128)}) custom-call(s32[4]{0:T(128)} %pad_add_fusion.meta_ref, s32[64]{0:T(128)} %get-tuple-element.21.row_ref, s32[64]{0:T(128)} %get-tuple-element.20.col_ref, s32[64,1]{1,0:T(8,128)} %copy.15.count_ref, s32[64,256]{1,0:T(8,128)} %ends_ref.1, ...), custom_call_target="tpu_custom_call" | custom-call | tf_op jit(solution)/shard_map/tiles/pallas_call | solution.py:173
  85.9 0.0 copy-start.1
  85.9 1.6 %copy-done.1 = f32[2048,256]{1,0:T(8,128)S(1)} copy-done((f32[2048,256]{1,0:T(8,128)S(1)}, f32[2048,256]{1,0:T(8,128)}, u32[]{:S(2)}) %copy-start.1) | copy-done | bytes 2097176
  87.5 0.0 copy-start.3
  87.5 1.2 copy-done.3
  88.7 50.2 %reduce.1 = (f32[256,256]{1,0:T(8,128)S(1)}, f32[256,256]{1,0:T(8,128)S(1)}, f32[2,4,4,32,256]{4,3,2,1,0:T(8,128)S(1)}) custom-call(f32[16,2,256,256]{3,2,1,0:T(8,128)} %bitcast.16, f32[8,256,256]{2,1,0:T(8,128)S(1)} %bitcast.11, f32[2,4,4,32,256]{4,3,2,1,0:T(8,128)S(1)} %bitcast.13), custom_call_target="tpu_custom_call" | custom-call | tf_op jit(solution)/shard_map/reduce/pallas_call | solution.py:622
  138.9 0.7 slice.8
  139.6 0.9 slice.9
  140.5 0.7 copy.19
  141.2 0.7 copy.20
Async XLA Ops:
  6.1 0.9 copy-start.4
  7.0 0.9 copy-start.5
  36.6 2.0 %copy-start = (bf16[32,256,256]{2,1,0:T(8,128)(2,1)}, bf16[32,256,256]{2,1,0:T(8,128)(2,1)S(1)}, u32[]{:S(2)}) copy-start(bf16[32,256,256]{2,1,0:T(8,128)(2,1)S(1)} %get-tuple-element.12) | copy-start | bytes 12582916
  38.6 1.0 copy-start.2
  85.9 1.6 %copy-start.1 = (f32[2048,256]{1,0:T(8,128)S(1)}, f32[2048,256]{1,0:T(8,128)}, u32[]{:S(2)}) copy-start(f32[2048,256]{1,0:T(8,128)} %get-tuple-element.15) | copy-start | bytes 6291460
  87.5 1.2 copy-start.3

commit v3 on v2

--- a/solution.py
+++ b/solution.py
@@ -13,6 +13,8 @@
 PAIR = 2 * TILE
 RELS_PAD = 256
 NONE = 1024
+UNROLL = 16
+VMEM_LIMIT = 60 * 1024 * 1024
 F32 = jnp.float32
 BF16 = jnp.bfloat16
 NN = (((1,), (0,)), ((), ()))
@@ -48,128 +50,209 @@
 
 
 def tiles_kernel(
-    meta_ref,
     row_ref,
     col_ref,
+    live_ref,
     count_ref,
     ends_ref,
     relation_ref,
     dir_ref,
-    feats_ref,
-    cot_ref,
     rel_ref,
     weights_ref,
-    grad_ref,
+    feats_any,
+    cot_any,
+    grad_any,
     mixed_ref,
     sums_ref,
     key_ref,
     src_ref,
+    feats_ref,
+    cot_ref,
+    turned_ref,
+    rel_pad_ref,
     totals_ref,
     counts_ref,
     high_ref,
     low_ref,
+    total_high_ref,
+    total_low_ref,
+    count_high_ref,
+    grad_ref,
+    self_rel_ref,
+    sems,
 ):
     slots = ends_ref.shape[0]
-    blocks = cot_ref.shape[0] // TILE
-    rels_all = meta_ref[3]
-    slot_iota = lax.broadcasted_iota(jnp.int32, (slots, EDGE_TILE), 0)
-    edge_iota = lax.broadcasted_iota(jnp.int32, (slots, EDGE_TILE), 1)
-    valid = (edge_iota < count_ref[...]) & (slot_iota < meta_ref[0])
+    dst_dev, src_dev = cot_ref.shape[0], feats_ref.shape[0]
+    blocks, source_blocks = dst_dev // TILE, src_dev // TILE
+    rels_all = rel_ref.shape[0]
+    col_index = row_ref[0] // blocks
+    row_index = col_ref[0] // source_blocks
+    ahead = col_index * blocks - row_index * source_blocks
+    owner = (ahead >= 0) & (ahead < source_blocks)
+    load_cot = pltpu.make_async_copy(cot_any, cot_ref, sems.at[0])
+    load_feats = pltpu.make_async_copy(feats_any, feats_ref, sems.at[1])
+    load_cot.start()
+    load_feats.start()
+
     ends = ends_ref[...]
-    key_ref[...] = jnp.where(valid, dir_ref[...] * TILE + lax.shift_right_logical(ends, 7), NONE)
+    key_ref[...] = dir_ref[...] * TILE + lax.shift_right_logical(ends, 7)
     src_ref[...] = ends & (TILE - 1)
-
+    rel_pad_ref[...] = jnp.zeros_like(rel_pad_ref)
+    rel_pad_ref[pl.ds(0, rels_all), :] = rel_ref[...]
     weight = [split(weights_ref[which]) for which in range(3)]
+
+    def clear_block(block, _):
+        grad_ref[rows_at(block, PAIR), :] = jnp.zeros((PAIR, D), F32)
+        return 0
+
+    lax.fori_loop(0, src_dev // PAIR, clear_block, 0)
+    sums_ref[pl.ds(2 * D, D), :] = jnp.zeros((D, D), F32)
+    self_rel_ref[...] = jnp.zeros_like(self_rel_ref)
+    load_cot.wait()
 
     def image_block(block, _):
         cot = cot_ref[rows_at(block, TILE), :]
-        pair = [dot_exact_left(cot, weight[which], NT) for which in range(2)]
-        high, low = split(jnp.concatenate(pair, axis=0))
+        turned_ref[:, rows_at(block, TILE)] = cot.T
         at = rows_at(block, PAIR)
-        high_ref[at, :] = high
-        low_ref[at, :] = low
+        for which in range(2):
+            high, low = split(dot_exact_left(cot, weight[which], NT))
+            part = pl.ds(pl.multiple_of(block * PAIR + which * TILE, TILE), TILE)
+            high_ref[part, :] = high
+            low_ref[part, :] = low
         totals_ref[at, :] = jnp.zeros((PAIR, D), F32)
         counts_ref[at, :] = jnp.zeros((PAIR, RELS_PAD), F32)
         return 0
 
-    lax.fori_loop(0, blocks, image_block, 0)
-
-    def clear_block(block, _):
-        grad_ref[rows_at(block, PAIR), :] = jnp.zeros((PAIR, D), F32)
-        return 0
-
-    lax.fori_loop(0, grad_ref.shape[0] // PAIR, clear_block, 0)
+    lax.fori_loop(0, blocks, image_block, 0, unroll=2)
+
+    @pl.when(owner)
+    def _():
+        def self_image(block, total):
+            image = dot_exact_left(cot_ref[rows_at(block, PAIR), :], weight[2], NT)
+            grad_ref[pl.ds(pl.multiple_of((ahead + 2 * block) * TILE, TILE), PAIR), :] = image
+            return total + jnp.sum(image.reshape(PAIR // 8, 8, D), axis=0)
+
+        self_rel_ref[...] = lax.fori_loop(0, blocks // 2, self_image, jnp.zeros((8, D), F32), unroll=2)
+
+    load_feats.wait()
 
     pair_iota = lax.broadcasted_iota(jnp.int32, (PAIR, EDGE_TILE), 0)
     tile_iota = lax.broadcasted_iota(jnp.int32, (TILE, EDGE_TILE), 0)
+    edge_iota = lax.broadcasted_iota(jnp.int32, (1, EDGE_TILE), 1)
 
     def hot(iota, entries):
         return jnp.where(iota == entries, 1.0, 0.0).astype(BF16)
 
     def tile(slot, _):
         at = pl.ds(slot, 1)
-        hot_dst = hot(pair_iota, key_ref[at, :])
+        edges = jnp.where(slot < live_ref[0], count_ref[slot], 0)
+        hot_dst = hot(pair_iota, jnp.where(edge_iota < edges, key_ref[at, :], NONE))
         hot_src = hot(tile_iota, src_ref[at, :])
         hot_rel = hot(pair_iota, relation_ref[at, :])
         forward = dot(hot_dst, hot_src, NT).astype(BF16)
         backward = dot(hot_src, hot_dst, NT).astype(BF16)
         counted = dot(hot_dst, hot_rel, NT)
-        row = rows_at(row_ref[slot], PAIR)
-        col = rows_at(col_ref[slot], TILE)
+        row = rows_at(row_ref[slot] % blocks, PAIR)
+        col = rows_at(col_ref[slot] % source_blocks, TILE)
+        totals_ref[row, :] += dot(forward, feats_ref[col, :])
         counts_ref[row, :] += counted
-        totals_ref[row, :] += dot(forward, feats_ref[col, :])
         grad_ref[col, :] += dot(backward, high_ref[row, :]) + dot(backward, low_ref[row, :])
         return 0
 
-    lax.fori_loop(0, slots, tile, 0, unroll=2)
-
-    relations = split(rel_ref[...])
-    sums_ref[...] = jnp.zeros_like(sums_ref)
-    weights_at = [pl.ds(which * D, D) for which in range(3)]
-    rel_at = pl.ds(3 * D, RELS_PAD)
+    lax.fori_loop(0, slots, tile, 0, unroll=UNROLL)
+
+    stores = []
+    for part in range(4):
+        here = pl.ds(part * (src_dev // 4), src_dev // 4)
+        copy = pltpu.make_async_copy(grad_ref.at[here, :], grad_any.at[here, :], sems.at[2 + part])
+        copy.start()
+        stores.append(copy)
+
+    relations = split(rel_pad_ref[...])
+
+    def most(block, value):
+        counts = counts_ref[rows_at(block, PAIR), :]
+        return jnp.maximum(value, jnp.max(counts.reshape(PAIR // 8, 8, RELS_PAD), axis=0))
+
+    largest = jnp.max(lax.fori_loop(0, blocks, most, jnp.zeros((8, RELS_PAD), F32)))
+    large = largest > 256.0
+
+    @pl.when(large)
+    def _():
+        def low_block(block, _):
+            at = rows_at(block, PAIR)
+            low = split(counts_ref[at, :])[1]
+            totals_ref[at, :] -= dot(low, relations[0]) + dot(low, relations[1])
+            return 0
+
+        lax.fori_loop(0, blocks, low_block, 0)
 
     def finish_block(block, _):
         at = rows_at(block, PAIR)
-        counts = split(counts_ref[at, :])
-        high, low = high_ref[at, :], low_ref[at, :]
-        rel_part = dot(counts[0], high, TN) + (dot(counts[0], low, TN) + dot(counts[1], high, TN))
-        sums_ref[rel_at, :] -= rel_part
-        totals = totals_ref[at, :] - dot_split(counts, relations)
-        total_in = split(totals[:TILE])
-        total_out = split(totals[TILE:])
         here = rows_at(block, TILE)
-        mixed_ref[here, :] = dot_split(total_in, weight[0]) + dot_split(total_out, weight[1])
-        cot = cot_ref[here, :]
-        sums_ref[weights_at[0], :] += dot_exact_right(total_in, cot, TN)
-        sums_ref[weights_at[1], :] += dot_exact_right(total_out, cot, TN)
+        counts = counts_ref[at, :].astype(BF16)
+        totals = totals_ref[at, :] - (dot(counts, relations[0]) + dot(counts, relations[1]))
+        pieces = [split(totals[:TILE]), split(totals[TILE:])]
+        for which in range(2):
+            total_high_ref[which, here, :] = pieces[which][0]
+            total_low_ref[which, here, :] = pieces[which][1]
+            count_high_ref[which, here, :] = counts[which * TILE : (which + 1) * TILE]
+        mixed_ref[here, :] = dot_split(pieces[0], weight[0]) + dot_split(pieces[1], weight[1])
         return 0
 
-    lax.fori_loop(0, blocks, finish_block, 0)
-
-    @pl.when(meta_ref[1] == 1)
+    lax.fori_loop(0, blocks, finish_block, 0, unroll=4)
+
+    turned = turned_ref[...]
+    grad_rel = jnp.zeros((D, RELS_PAD), F32)
+    met = [dot(turned, count_high_ref[which]) for which in range(2)]
+    for which in range(2):
+        product = dot(turned, total_high_ref[which]) + dot(turned, total_low_ref[which])
+        sums_ref[pl.ds(which * D, D), :] = product.T
+        grad_rel -= dot_split(weight[which], split(met[which]))
+    sums_ref[pl.ds(3 * D, RELS_PAD), :] = grad_rel.T
+
+    @pl.when(large)
+    def _():
+        def low_block(block, _):
+            cot = cot_ref[rows_at(block, TILE), :]
+            counts = counts_ref[rows_at(block, PAIR), :]
+            for which in range(2):
+                low = split(counts[which * TILE : (which + 1) * TILE])[1]
+                part = split(dot(low, cot, TN))
+                sums_ref[pl.ds(3 * D, RELS_PAD), :] -= dot_split(part, weight[which], NT)
+            return 0
+
+        lax.fori_loop(0, blocks, low_block, 0)
+
+    sums_ref[pl.ds(3 * D + rels_all - 1, 1), :] -= jnp.sum(self_rel_ref[...], axis=0, keepdims=True)
+
+    @pl.when(owner)
     def _():
         own_rel = rel_ref[pl.ds(rels_all - 1, 1), :]
 
-        def self_block(block, total):
-            here = rows_at(block, TILE)
-            there = rows_at(meta_ref[2] + block, TILE)
+        def self_block(block, _):
+            here = rows_at(block, PAIR)
+            there = pl.ds(pl.multiple_of((ahead + 2 * block) * TILE, TILE), PAIR)
             self_term = split(feats_ref[there, :].astype(F32) - own_rel)
-            cot = cot_ref[here, :]
+            total_high_ref[0, here, :] = self_term[0]
+            total_low_ref[0, here, :] = self_term[1]
             mixed_ref[here, :] += dot_split(self_term, weight[2])
-            sums_ref[weights_at[2], :] += dot_exact_right(self_term, cot, TN)
-            image = dot_exact_left(cot, weight[2], NT)
-            grad_ref[there, :] += image
-            return total + jnp.sum(image, axis=0, keepdims=True)
-
-        total = lax.fori_loop(0, blocks, self_block, jnp.zeros((1, D), F32))
-        sums_ref[pl.ds(3 * D + rels_all - 1, 1), :] -= total
-
-
-def tiles_call(meta, rows, cols, counts, ends, relation, direction, sources, cot, rel, weights):
+            return 0
+
+        lax.fori_loop(0, blocks // 2, self_block, 0, unroll=2)
+        product = dot(turned, total_high_ref[0]) + dot(turned, total_low_ref[0])
+        sums_ref[pl.ds(2 * D, D), :] = product.T
+
+    for copy in stores:
+        copy.wait()
+
+
+def tiles_call(rows, cols, live, counts, ends, relation, direction, rel, weights, sources, cot):
     dst_dev, src_dev = cot.shape[0], sources.shape[0]
     slots = ends.shape[0]
     smem = pl.BlockSpec(memory_space=pltpu.SMEM)
     vmem = pl.BlockSpec(memory_space=pltpu.VMEM)
+    anywhere = pl.BlockSpec(memory_space=pl.ANY)
     return pl.pallas_call(
         tiles_kernel,
         out_shape=[
@@ -177,19 +260,29 @@
             jax.ShapeDtypeStruct((dst_dev, D), F32),
             jax.ShapeDtypeStruct((3 * D + RELS_PAD, D), F32),
         ],
-        in_specs=[smem] * 3 + [vmem] * 8,
-        out_specs=[vmem] * 3,
+        in_specs=[smem] * 4 + [vmem] * 5 + [anywhere] * 2,
+        out_specs=[anywhere, vmem, vmem],
         scratch_shapes=[
             pltpu.VMEM((slots, EDGE_TILE), jnp.int32),
             pltpu.VMEM((slots, EDGE_TILE), jnp.int32),
+            pltpu.VMEM((src_dev, D), BF16),
+            pltpu.VMEM((dst_dev, D), BF16),
+            pltpu.VMEM((D, dst_dev), BF16),
+            pltpu.VMEM((RELS_PAD, D), F32),
             pltpu.VMEM((2 * dst_dev, D), F32),
             pltpu.VMEM((2 * dst_dev, RELS_PAD), F32),
             pltpu.VMEM((2 * dst_dev, D), BF16),
             pltpu.VMEM((2 * dst_dev, D), BF16),
+            pltpu.VMEM((2, dst_dev, D), BF16),
+            pltpu.VMEM((2, dst_dev, D), BF16),
+            pltpu.VMEM((2, dst_dev, RELS_PAD), BF16),
+            pltpu.VMEM((src_dev, D), F32),
+            pltpu.VMEM((8, D), F32),
+            pltpu.SemaphoreType.DMA((6,)),
         ],
-        compiler_params=pltpu.CompilerParams(vmem_limit_bytes=56 * 1024 * 1024),
+        compiler_params=pltpu.CompilerParams(vmem_limit_bytes=VMEM_LIMIT),
         name="tiles",
-    )(meta, rows, cols, counts, ends, relation, direction, sources, cot, rel, weights)
+    )(rows, cols, live, counts, ends, relation, direction, rel, weights, sources, cot)
 
 
 MESH = pl.DeviceIdType.MESH
@@ -265,7 +358,17 @@
             pass
 
 
-def gather_kernel(rows, feats_ref, cot_ref, sources_ref, targets_ref, send_sems, shard_sems, row_sems, own_sems):
+def gather_kernel(
+    rows,
+    feats_ref,
+    cot_ref,
+    sources_ref,
+    targets_ref,
+    send_sems,
+    shard_sems,
+    row_sems,
+    own_sems,
+):
     place = Place()
     copies = Copies(send_sems)
     copies.any_peer = place.partner()
@@ -388,15 +491,14 @@
 
 def gather_call(feats, cot, rows, cols):
     anywhere = pl.BlockSpec(memory_space=pl.ANY)
-    vmem = pl.BlockSpec(memory_space=pltpu.VMEM)
     sources, targets = pl.pallas_call(
         functools.partial(gather_kernel, rows),
         out_shape=[
             jax.ShapeDtypeStruct((cols,) + feats.shape, feats.dtype),
             jax.ShapeDtypeStruct((rows,) + cot.shape, cot.dtype),
         ],
-        in_specs=[vmem, vmem],
-        out_specs=[anywhere, anywhere],
+        in_specs=[anywhere] * 2,
+        out_specs=[anywhere] * 2,
         scratch_shapes=[
             pltpu.SemaphoreType.DMA((160,)),
             pltpu.SemaphoreType.DMA((2 * cols,)),
@@ -404,7 +506,7 @@
             pltpu.SemaphoreType.DMA((2,)),
         ],
         compiler_params=pltpu.CompilerParams(
-            collective_id=0, has_side_effects=True, vmem_limit_bytes=32 * 1024 * 1024
+            collective_id=0, has_side_effects=True, vmem_limit_bytes=VMEM_LIMIT
         ),
         name="gather",
     )(feats, cot)
@@ -414,12 +516,14 @@
 def reduce_kernel(
     rows,
     grad_any,
-    mixed_in,
-    sums_in,
+    mixed_any,
+    sums_any,
     grad_out,
     mixed_out,
     sums_out,
     grad_acc,
+    mixed_in,
+    sums_in,
     pair_in,
     relay1,
     ring1,
@@ -446,6 +550,10 @@
     partner = place.partner()
     core = place.core
     order1 = (2, 1, 3, 0)
+    load_sums = pltpu.make_async_copy(sums_any.at[core], sums_in, own_sems.at[16])
+    load_mixed = pltpu.make_async_copy(mixed_any, mixed_in, own_sems.at[17])
+    load_sums.start()
+    load_mixed.start()
     own_copies = {}
     for k in order1:
         for r in (2, 1, 3, 0):
@@ -535,9 +643,10 @@
 
     def mixed_pipe():
         after, before = place.along_row(1, rows), place.along_row(rows - 1, rows)
-        copies.start(mixed_in.at[(place.row + rows - 1) % rows, low], row_up.at[0], row_sems.at[0], after)
-        copies.start(mixed_in.at[(place.row + 1) % rows, high], row_down.at[0], row_sems.at[rows], before)
-        yield
+        copies.start(mixed_any.at[(place.row + rows - 1) % rows, low], row_up.at[0], row_sems.at[0], after)
+        copies.start(mixed_any.at[(place.row + 1) % rows, high], row_down.at[0], row_sems.at[rows], before)
+        yield
+        load_mixed.wait()
         for step in range(1, rows):
             copies.received(row_up.at[step - 1], row_sems.at[step - 1])
             row_up[step - 1] += mixed_in[(place.row + 2 * rows - 1 - step) % rows, low]
@@ -552,11 +661,12 @@
         mixed_out[high] = row_down[rows - 2]
 
     def sums_pipe():
-        copies.start(sums_in.at[1 - core], sum_pair, sum_sems.at[0], partner)
-        yield
+        copies.start(sums_any.at[1 - core], sum_pair, sum_sems.at[0], partner)
+        yield
+        load_sums.wait()
         copies.received(sum_pair, sum_sems.at[0])
         for q in range(RING):
-            sum_pair[q] += sums_in[core, q]
+            sum_pair[q] += sums_in[q]
         for k in (2, 1, 3):
             copies.start(sum_pair.at[(place.p1 + k) % RING], sum_first.at[k], sum_sems.at[k], place.peer(k, 0))
         sum_first[0] = sum_pair[place.p1]
@@ -595,20 +705,28 @@
         for quarter in range(RING):
             for side in range(2):
                 own[pl.ds(8 * quarter, 8), pl.ds(TILE * side, TILE)] = sum_tiles[rows + 2 * quarter + side]
-        others = [(k1, k2) for k1 in range(RING) for k2 in range(RING) if k1 or k2]
-        for k1, k2 in others:
-            copies.start(own, own, spread_sems.at[4 * k1 + k2], place.peer(k1, k2))
-        yield
-        for k1, k2 in others:
-            there = sums_out.at[core, (place.p1 + RING - k1) % RING, (place.p2 + RING - k2) % RING]
-            copies.received(there, spread_sems.at[4 * k1 + k2])
-        copies.start(sums_out.at[core], sums_out.at[core], spread_sems.at[0], partner)
-        yield
-        copies.received(sums_out.at[1 - core], spread_sems.at[0])
+        for k in (2, 1, 3):
+            copies.start(own, own, spread_sems.at[k], place.peer(0, k))
+        yield
+        for k in (1, 3, 2):
+            copies.received(sums_out.at[core, place.p1, (place.p2 + RING - k) % RING], spread_sems.at[k])
+        line = sums_out.at[core, place.p1]
+        for k in (2, 1, 3):
+            copies.start(line, line, spread_sems.at[3 + k], place.peer(k, 0))
+        yield
+        copies.start(line, line, spread_sems.at[7], partner)
+        for k in (1, 3, 2):
+            there = sums_out.at[core, (place.p1 + RING - k) % RING]
+            copies.received(there, spread_sems.at[3 + k])
+            copies.start(there, there, spread_sems.at[7 + k], partner)
+        yield
+        copies.received(sums_out.at[1 - core, place.p2], spread_sems.at[7])
+        for k in (1, 3, 2):
+            copies.received(sums_out.at[1 - core, (place.p2 + RING - k) % RING], spread_sems.at[7 + k])
 
     run_in_order(
         {"s": sums_pipe(), "m": mixed_pipe(), "g": grad_pipe()},
-        "smg" + "s" + "g" + "m" + "s" + "g" + "m" + "s" + "g" + "s" + "m" + "g" + "s" + "m" + "g" + "m" + "s" + "g" + "m" + "g" + "m" + "s" + "g",
+        "smgsmgsmgsmgsmgsmgsmgsmgmg",
     )
     copies.finish()
 
@@ -626,10 +744,12 @@
             jax.ShapeDtypeStruct(block, F32),
             jax.ShapeDtypeStruct((2, RING, RING, share, D), F32),
         ],
-        in_specs=[anywhere, vmem, vmem],
+        in_specs=[anywhere] * 3,
         out_specs=[vmem] * 3,
         scratch_shapes=[
             pltpu.VMEM((RING, RING) + block, F32),
+            pltpu.VMEM((rows,) + block, F32),
+            pltpu.VMEM((RING, RING, share, D), F32),
             pltpu.VMEM((RING, RING) + block, F32),
             pltpu.VMEM((2, 2) + block, F32),
             pltpu.VMEM((2, RING) + block, F32),
@@ -643,7 +763,7 @@
             pltpu.VMEM((rows, 8, TILE), F32),
             pltpu.VMEM((2 * rows, 8, TILE), F32),
             pltpu.SemaphoreType.DMA((96,)),
-            pltpu.SemaphoreType.DMA((16,)),
+            pltpu.SemaphoreType.DMA((18,)),
             pltpu.SemaphoreType.DMA((16,)),
             pltpu.SemaphoreType.DMA((12,)),
             pltpu.SemaphoreType.DMA((2 * rows,)),
@@ -677,29 +797,21 @@
 ):
     rows_n = lax.axis_size("row")
     cols_n = lax.axis_size("col")
-    row_index = lax.axis_index("row")
-    col_index = lax.axis_index("col")
-    ent_dev = feats.shape[0]
-    src_dev = ent_dev * cols_n
-    dst_dev = ent_dev * rows_n
-    rels_all = rel_embed.shape[0]
     sources, targets = gather_call(feats, cot, rows_n, cols_n)
-    owner = (row_index == col_index * rows_n // cols_n).astype(jnp.int32)
-    offset = jnp.clip(col_index * dst_dev - row_index * src_dev, 0, src_dev - dst_dev) // TILE
-    meta = jnp.stack([tile_live[0], owner, offset.astype(jnp.int32), jnp.int32(rels_all)])
     grad, mixed, sums = tiles_call(
-        meta,
-        tile_row - col_index * (dst_dev // TILE),
-        tile_col - row_index * (src_dev // TILE),
-        edge_count[:, None],
+        tile_row,
+        tile_col,
+        tile_live,
+        edge_count,
         edge_ends,
         edge_relation,
         edge_dir,
+        rel_embed,
+        weights,
         sources,
         targets,
-        jnp.pad(rel_embed, ((0, RELS_PAD - rels_all), (0, 0))),
-        weights,
     )
+    rels_all = rel_embed.shape[0]
     grad_feats, mixed, sums = reduce_call(grad, mixed, sums, rows_n, cols_n)
     grad_rel = sums[3 * D : 3 * D + rels_all]
     return (mixed, grad_feats, grad_rel, sums[: 3 * D].reshape(3, D, D))

time: 145 us -> 115 us (0.79); the launches traced: 142 us -> 115 us
  Pallas kernels: 125 us -> 108 us
  local copies, waits for them, and re-layouts: 13.6 us -> 5.84 us
  other arithmetic: 1.79 us -> 0 us
    pallas_call x1, Pallas kernels: 46.3 us -> 29.6 us  [tiles_call(): pl.pallas_call(tiles_kernel, out_shape=[jax.ShapeDtypeStruct((src_dev, D)...]
    unnamed x14 -> x6, local copies, waits for them, and re-layouts: 8.97 us -> 4.21 us
    pallas_call x1, Pallas kernels: 50.2 us -> 48.1 us  [reduce_call(): pl.pallas_call(functools.partial(reduce_kernel, rows), out_shape=[jax.Sha...]
    pad x1 -> x0, local copies, waits for them, and re-layouts: 1.65 us -> none  [shards(): jnp.pad(rel_embed, ((0, RELS_PAD - rels_all), (0, 0)))]
where the time goes in v3:
time: 115 us
  Pallas kernels  108 us (94%)
  local copies, waits for them, and re-layouts  5.84 us (5%)
  between operations  1.31 us (1%)
    pallas_call x1, Pallas kernels, reduce_call(): pl.pallas_call(functools.partial(reduce_kernel, rows), out_shape=[jax.Sha...  48.1 us
    pallas_call x1, Pallas kernels, gather_call(): pl.pallas_call(functools.partial(gather_kernel, rows), out_shape=[jax.Sha...  29.9 us
    pallas_call x1, Pallas kernels, tiles_call(): pl.pallas_call(tiles_kernel, out_shape=[jax.ShapeDtypeStruct((src_dev, D)...  29.6 us
    unnamed x6, local copies, waits for them, and re-layouts  4.21 us

profile of v3, /device:TPU:6, one launch (start us, length us, event | category | flops | bytes accessed | tf_op | source)
XLA Modules:
  0.0 114.8 jit_solution(4595566975895687427)
XLA Ops:
  1.3 29.9 %gather.1 = (bf16[32,256,256]{2,1,0:T(8,128)(2,1)}, bf16[8,256,256]{2,1,0:T(8,128)(2,1)}) custom-call(bf16[256,256]{1,0:T(8,128)(2,1)} %feats_ref.1, bf16[256,256]{1,0:T(8,128)(2,1)} %cot_ref.1), custom_call_target="tpu_custom_call" | custom-call | tf_op jit(solution)/shard_map/gather/pallas_call | solution.py:494
  31.2 29.6 %tiles.1 = (f32[8192,256]{1,0:T(8,128)}, f32[2048,256]{1,0:T(8,128)}, f32[1024,256]{1,0:T(8,128)}) custom-call(s32[64]{0:T(128)} %row_ref.1, s32[64]{0:T(128)} %col_ref.1, s32[1]{0:T(128)S(6)} %copy.17.live_ref, s32[64]{0:T(128)} %count_ref.1, s32[64,256]{1,0:T(8,128)} %ends_ref.1, s32[64,256]{1,0:T(8,128)} %relation_ref.1, s32[64,256]{1,0:T(8,128)} %dir_ref.1, ...), custom_call_target="tpu_custom_call" | custom-call | tf_op jit(solution)/shard_map/tiles/pallas_call | solution.py:256
  60.8 0.0 copy-start
  60.8 1.6 %copy-done = f32[2048,256]{1,0:T(8,128)S(1)} copy-done((f32[2048,256]{1,0:T(8,128)S(1)}, f32[2048,256]{1,0:T(8,128)}, u32[]{:S(2)}) %copy-start) | copy-done | bytes 2097176
  62.4 0.0 copy-start.1
  62.4 1.2 %copy-done.1 = f32[1024,256]{1,0:T(8,128)S(1)} copy-done((f32[1024,256]{1,0:T(8,128)S(1)}, f32[1024,256]{1,0:T(8,128)}, u32[]{:S(2)}) %copy-start.1) | copy-done | bytes 1048600
  63.6 48.1 %reduce.1 = (f32[256,256]{1,0:T(8,128)S(1)}, f32[256,256]{1,0:T(8,128)S(1)}, f32[2,4,4,32,256]{4,3,2,1,0:T(8,128)S(1)}) custom-call(f32[16,2,256,256]{3,2,1,0:T(8,128)} %bitcast.11, f32[8,256,256]{2,1,0:T(8,128)S(1)} %bitcast.7, f32[2,4,4,32,256]{4,3,2,1,0:T(8,128)S(1)} %bitcast.8), custom_call_target="tpu_custom_call" | custom-call | tf_op jit(solution)/shard_map/reduce/pallas_call | solution.py:740
  111.8 0.7 slice.8
  112.5 0.9 slice.9
  113.4 0.7 copy.18
  114.1 0.7 copy.19
Async XLA Ops:
  60.8 1.6 %copy-start = (f32[2048,256]{1,0:T(8,128)S(1)}, f32[2048,256]{1,0:T(8,128)}, u32[]{:S(2)}) copy-start(f32[2048,256]{1,0:T(8,128)} %get-tuple-element.15) | copy-start | bytes 6291460
  62.4 1.2 %copy-start.1 = (f32[1024,256]{1,0:T(8,128)S(1)}, f32[1024,256]{1,0:T(8,128)}, u32[]{:S(2)}) copy-start(f32[1024,256]{1,0:T(8,128)} %get-tuple-element.16) | copy-start | bytes 3145732

commit v4 on v3

--- a/solution.py
+++ b/solution.py
@@ -13,8 +13,11 @@
 PAIR = 2 * TILE
 RELS_PAD = 256
 NONE = 1024
-UNROLL = 16
-VMEM_LIMIT = 60 * 1024 * 1024
+CHUNKS = 8
+PREPARED = 16
+GATHER_VMEM = 60 * 1024 * 1024
+TILES_VMEM = 60 * 1024 * 1024
+REDUCE_VMEM = 52 * 1024 * 1024
 F32 = jnp.float32
 BF16 = jnp.bfloat16
 NN = (((1,), (0,)), ((), ()))
@@ -49,23 +52,26 @@
     return pl.ds(pl.multiple_of(index * size, size), size)
 
 
+def hot(iota, entries):
+    return jnp.where(iota == entries, 1.0, 0.0).astype(BF16)
+
+
 def tiles_kernel(
     row_ref,
     col_ref,
-    live_ref,
-    count_ref,
-    ends_ref,
-    relation_ref,
-    dir_ref,
     rel_ref,
     weights_ref,
     feats_any,
     cot_any,
+    forward_any,
+    backward_any,
+    counted_any,
     grad_any,
     mixed_ref,
     sums_ref,
-    key_ref,
-    src_ref,
+    forward_ref,
+    backward_ref,
+    counted_ref,
     feats_ref,
     cot_ref,
     turned_ref,
@@ -74,14 +80,12 @@
     counts_ref,
     high_ref,
     low_ref,
-    total_high_ref,
-    total_low_ref,
     count_high_ref,
     grad_ref,
     self_rel_ref,
     sems,
 ):
-    slots = ends_ref.shape[0]
+    slots = forward_ref.shape[0]
     dst_dev, src_dev = cot_ref.shape[0], feats_ref.shape[0]
     blocks, source_blocks = dst_dev // TILE, src_dev // TILE
     rels_all = rel_ref.shape[0]
@@ -94,9 +98,16 @@
     load_cot.start()
     load_feats.start()
 
-    ends = ends_ref[...]
-    key_ref[...] = dir_ref[...] * TILE + lax.shift_right_logical(ends, 7)
-    src_ref[...] = ends & (TILE - 1)
+    chunk = slots // CHUNKS
+    loads = []
+    for part in range(CHUNKS):
+        here = pl.ds(part * chunk, chunk)
+        for which, (src, dst) in enumerate(
+            ((forward_any, forward_ref), (backward_any, backward_ref), (counted_any, counted_ref))
+        ):
+            copy = pltpu.make_async_copy(src.at[here], dst.at[here], sems.at[6 + 3 * part + which])
+            copy.start()
+            loads.append(copy)
     rel_pad_ref[...] = jnp.zeros_like(rel_pad_ref)
     rel_pad_ref[pl.ds(0, rels_all), :] = rel_ref[...]
     weight = [split(weights_ref[which]) for which in range(3)]
@@ -121,6 +132,7 @@
             low_ref[part, :] = low
         totals_ref[at, :] = jnp.zeros((PAIR, D), F32)
         counts_ref[at, :] = jnp.zeros((PAIR, RELS_PAD), F32)
+        mixed_ref[rows_at(block, TILE), :] = jnp.zeros((TILE, D), F32)
         return 0
 
     lax.fori_loop(0, blocks, image_block, 0, unroll=2)
@@ -136,30 +148,38 @@
 
     load_feats.wait()
 
-    pair_iota = lax.broadcasted_iota(jnp.int32, (PAIR, EDGE_TILE), 0)
-    tile_iota = lax.broadcasted_iota(jnp.int32, (TILE, EDGE_TILE), 0)
-    edge_iota = lax.broadcasted_iota(jnp.int32, (1, EDGE_TILE), 1)
-
-    def hot(iota, entries):
-        return jnp.where(iota == entries, 1.0, 0.0).astype(BF16)
+    @pl.when(owner)
+    def _():
+        own_rel = rel_ref[pl.ds(rels_all - 1, 1), :]
+
+        def self_block(block, _):
+            here = rows_at(block, PAIR)
+            there = pl.ds(pl.multiple_of((ahead + 2 * block) * TILE, TILE), PAIR)
+            self_term = split(feats_ref[there, :].astype(F32) - own_rel)
+            count_high_ref[0, here, :] = self_term[0]
+            count_high_ref[1, here, :] = self_term[1]
+            mixed_ref[here, :] = dot_split(self_term, weight[2])
+            return 0
+
+        lax.fori_loop(0, blocks // 2, self_block, 0, unroll=2)
+        turned = turned_ref[...]
+        product = dot(turned, count_high_ref[0]) + dot(turned, count_high_ref[1])
+        sums_ref[pl.ds(2 * D, D), :] = product.T
+
 
     def tile(slot, _):
-        at = pl.ds(slot, 1)
-        edges = jnp.where(slot < live_ref[0], count_ref[slot], 0)
-        hot_dst = hot(pair_iota, jnp.where(edge_iota < edges, key_ref[at, :], NONE))
-        hot_src = hot(tile_iota, src_ref[at, :])
-        hot_rel = hot(pair_iota, relation_ref[at, :])
-        forward = dot(hot_dst, hot_src, NT).astype(BF16)
-        backward = dot(hot_src, hot_dst, NT).astype(BF16)
-        counted = dot(hot_dst, hot_rel, NT)
         row = rows_at(row_ref[slot] % blocks, PAIR)
         col = rows_at(col_ref[slot] % source_blocks, TILE)
-        totals_ref[row, :] += dot(forward, feats_ref[col, :])
-        counts_ref[row, :] += counted
+        backward = backward_ref[slot]
+        totals_ref[row, :] += dot(forward_ref[slot], feats_ref[col, :])
+        counts_ref[row, :] += counted_ref[slot].astype(F32)
         grad_ref[col, :] += dot(backward, high_ref[row, :]) + dot(backward, low_ref[row, :])
         return 0
 
-    lax.fori_loop(0, slots, tile, 0, unroll=UNROLL)
+    for part in range(CHUNKS):
+        for copy in loads[3 * part : 3 * part + 3]:
+            copy.wait()
+        lax.fori_loop(part * chunk, (part + 1) * chunk, tile, 0, unroll=True)
 
     stores = []
     for part in range(4):
@@ -194,10 +214,11 @@
         totals = totals_ref[at, :] - (dot(counts, relations[0]) + dot(counts, relations[1]))
         pieces = [split(totals[:TILE]), split(totals[TILE:])]
         for which in range(2):
-            total_high_ref[which, here, :] = pieces[which][0]
-            total_low_ref[which, here, :] = pieces[which][1]
+            there = pl.ds(pl.multiple_of(which * dst_dev + block * TILE, TILE), TILE)
+            high_ref[there, :] = pieces[which][0]
+            low_ref[there, :] = pieces[which][1]
             count_high_ref[which, here, :] = counts[which * TILE : (which + 1) * TILE]
-        mixed_ref[here, :] = dot_split(pieces[0], weight[0]) + dot_split(pieces[1], weight[1])
+        mixed_ref[here, :] += dot_split(pieces[0], weight[0]) + dot_split(pieces[1], weight[1])
         return 0
 
     lax.fori_loop(0, blocks, finish_block, 0, unroll=4)
@@ -206,7 +227,8 @@
     grad_rel = jnp.zeros((D, RELS_PAD), F32)
     met = [dot(turned, count_high_ref[which]) for which in range(2)]
     for which in range(2):
-        product = dot(turned, total_high_ref[which]) + dot(turned, total_low_ref[which])
+        there = pl.ds(which * dst_dev, dst_dev)
+        product = dot(turned, high_ref[there, :]) + dot(turned, low_ref[there, :])
         sums_ref[pl.ds(which * D, D), :] = product.T
         grad_rel -= dot_split(weight[which], split(met[which]))
     sums_ref[pl.ds(3 * D, RELS_PAD), :] = grad_rel.T
@@ -226,30 +248,12 @@
 
     sums_ref[pl.ds(3 * D + rels_all - 1, 1), :] -= jnp.sum(self_rel_ref[...], axis=0, keepdims=True)
 
-    @pl.when(owner)
-    def _():
-        own_rel = rel_ref[pl.ds(rels_all - 1, 1), :]
-
-        def self_block(block, _):
-            here = rows_at(block, PAIR)
-            there = pl.ds(pl.multiple_of((ahead + 2 * block) * TILE, TILE), PAIR)
-            self_term = split(feats_ref[there, :].astype(F32) - own_rel)
-            total_high_ref[0, here, :] = self_term[0]
-            total_low_ref[0, here, :] = self_term[1]
-            mixed_ref[here, :] += dot_split(self_term, weight[2])
-            return 0
-
-        lax.fori_loop(0, blocks // 2, self_block, 0, unroll=2)
-        product = dot(turned, total_high_ref[0]) + dot(turned, total_low_ref[0])
-        sums_ref[pl.ds(2 * D, D), :] = product.T
-
     for copy in stores:
         copy.wait()
 
 
-def tiles_call(rows, cols, live, counts, ends, relation, direction, rel, weights, sources, cot):
+def tiles_call(rows, cols, rel, weights, sources, cot, forward, backward, counted):
     dst_dev, src_dev = cot.shape[0], sources.shape[0]
-    slots = ends.shape[0]
     smem = pl.BlockSpec(memory_space=pltpu.SMEM)
     vmem = pl.BlockSpec(memory_space=pltpu.VMEM)
     anywhere = pl.BlockSpec(memory_space=pl.ANY)
@@ -260,11 +264,12 @@
             jax.ShapeDtypeStruct((dst_dev, D), F32),
             jax.ShapeDtypeStruct((3 * D + RELS_PAD, D), F32),
         ],
-        in_specs=[smem] * 4 + [vmem] * 5 + [anywhere] * 2,
+        in_specs=[smem] * 2 + [vmem] * 2 + [anywhere] * 5,
         out_specs=[anywhere, vmem, vmem],
         scratch_shapes=[
-            pltpu.VMEM((slots, EDGE_TILE), jnp.int32),
-            pltpu.VMEM((slots, EDGE_TILE), jnp.int32),
+            pltpu.VMEM(forward.shape, BF16),
+            pltpu.VMEM(backward.shape, BF16),
+            pltpu.VMEM(counted.shape, BF16),
             pltpu.VMEM((src_dev, D), BF16),
             pltpu.VMEM((dst_dev, D), BF16),
             pltpu.VMEM((D, dst_dev), BF16),
@@ -273,16 +278,14 @@
             pltpu.VMEM((2 * dst_dev, RELS_PAD), F32),
             pltpu.VMEM((2 * dst_dev, D), BF16),
             pltpu.VMEM((2 * dst_dev, D), BF16),
-            pltpu.VMEM((2, dst_dev, D), BF16),
-            pltpu.VMEM((2, dst_dev, D), BF16),
             pltpu.VMEM((2, dst_dev, RELS_PAD), BF16),
             pltpu.VMEM((src_dev, D), F32),
             pltpu.VMEM((8, D), F32),
-            pltpu.SemaphoreType.DMA((6,)),
+            pltpu.SemaphoreType.DMA((6 + 3 * CHUNKS,)),
         ],
-        compiler_params=pltpu.CompilerParams(vmem_limit_bytes=VMEM_LIMIT),
+        compiler_params=pltpu.CompilerParams(vmem_limit_bytes=TILES_VMEM),
         name="tiles",
-    )(rows, cols, live, counts, ends, relation, direction, rel, weights, sources, cot)
+    )(rows, cols, rel, weights, sources, cot, forward, backward, counted)
 
 
 MESH = pl.DeviceIdType.MESH
@@ -360,14 +363,26 @@
 
 def gather_kernel(
     rows,
+    live_ref,
+    count_ref,
+    ends_ref,
+    relation_ref,
+    dir_ref,
     feats_ref,
     cot_ref,
     sources_ref,
     targets_ref,
+    forward_any,
+    backward_any,
+    counted_any,
+    forward_ref,
+    backward_ref,
+    counted_ref,
     send_sems,
     shard_sems,
     row_sems,
     own_sems,
+    tile_sems,
 ):
     place = Place()
     copies = Copies(send_sems)
@@ -386,56 +401,54 @@
     )
     parts = [pl.ds(0, HALF), pl.ds(HALF, HALF)]
 
-    def send_shard(b, which, peer, src=None):
-        for half in which:
-            here = sources_ref.at[b, parts[half]]
-            copies.start(here if src is None else src.at[parts[half]], here, shard_sems.at[2 * b + half], peer)
-
-    def got_shard(b, which):
-        for half in which:
-            copies.received(sources_ref.at[b, parts[half]], shard_sems.at[2 * b + half])
+    def send(array, sems, count, index, peer, half=None, src=None):
+        here = array.at[index] if half is None else array.at[index, parts[half]]
+        sem = sems.at[2 * count + index] if half is None else sems.at[2 * index + half]
+        copies.start(here if src is None else src, here, sem, peer)
+
+    def got(array, sems, count, index, halves=False):
+        if halves:
+            for half in range(2):
+                copies.received(array.at[index, parts[half]], sems.at[2 * index + half])
+        else:
+            copies.received(array.at[index], sems.at[2 * count + index])
+
+    send_shard = functools.partial(send, sources_ref, shard_sems, 2 * RING * RING)
+    got_shard = functools.partial(got, sources_ref, shard_sems, 2 * RING * RING)
+    send_row = functools.partial(send, targets_ref, row_sems, rows)
+    got_row = functools.partial(got, targets_ref, row_sems, rows)
 
     def feats_pipe():
-        for half in (0, 1):
-            for peer in (place.peer(1, 0), place.peer(3, 0)):
-                send_shard(place.col, [half], peer, feats_ref)
-        for peer in (place.peer(0, 1), place.peer(0, 3), place.partner()):
-            send_shard(place.col, [0, 1], peer, feats_ref)
-        yield
-
-        def spread(b, which):
-            for peer in (place.peer(0, 1), place.peer(0, 3)):
-                send_shard(b, which, peer)
-            send_shard(b, which, place.partner())
+        for peer in (place.peer(1, 0), place.peer(3, 0), place.peer(0, 1), place.peer(0, 3), place.partner()):
+            send_shard(place.col, peer, src=feats_ref)
+        yield
+
+        def spread(b):
+            for peer in (place.peer(0, 1), place.peer(0, 3), place.partner()):
+                send_shard(b, peer)
 
         left, right, far = place.col_at(3, 0), place.col_at(1, 0), place.col_at(2, 0)
-        got_shard(left, [0])
-        send_shard(left, [0], place.peer(1, 0))
-        spread(left, [0])
-        got_shard(right, [0])
-        spread(right, [0])
-        got_shard(right, [1])
-        send_shard(right, [1], place.peer(3, 0))
-        spread(right, [1])
-        got_shard(left, [1])
-        spread(left, [1])
+        got_shard(left)
+        send_shard(left, place.peer(1, 0), 0)
+        spread(left)
+        got_shard(right)
+        send_shard(right, place.peer(3, 0), 1)
+        spread(right)
         yield
 
         def second(k1):
             below, above = place.col_at(k1, 3), place.col_at(k1, 1)
-            got_shard(below, [0])
-            send_shard(below, [0], place.peer(0, 1))
-            got_shard(above, [0])
-            got_shard(above, [1])
-            send_shard(above, [1], place.peer(0, 3))
-            got_shard(below, [1])
-            send_shard(below, [0, 1], place.partner())
-            send_shard(above, [0, 1], place.partner())
+            got_shard(below)
+            send_shard(below, place.peer(0, 1), 0)
+            got_shard(above)
+            send_shard(above, place.peer(0, 3), 1)
+            send_shard(below, place.partner())
+            send_shard(above, place.partner())
 
         second(0)
         yield
-        got_shard(far, [0, 1])
-        spread(far, [0, 1])
+        got_shard(far, halves=True)
+        spread(far)
         yield
         second(3)
         yield
@@ -445,72 +458,96 @@
         yield
         for k1 in (0, 3, 1, 2):
             b = place.col_at(k1, 2)
-            got_shard(b, [0, 1])
-            send_shard(b, [0, 1], place.partner())
+            got_shard(b, halves=True)
+            send_shard(b, place.partner())
         yield
         for k1 in range(RING):
             for k2 in range(RING):
-                got_shard(place.col_at(k1, k2) + 1 - 2 * place.core, [0, 1])
+                got_shard(place.col_at(k1, k2) + 1 - 2 * place.core)
 
     def cot_pipe():
         after, before = place.along_row(1, rows), place.along_row(rows - 1, rows)
-
-        def send_row(index, which, peer, src=None):
-            for half in which:
-                here = targets_ref.at[index, parts[half]]
-                copies.start(here if src is None else src.at[parts[half]], here, row_sems.at[2 * index + half], peer)
-
-        def got_row(index, which):
-            for half in which:
-                copies.received(targets_ref.at[index, parts[half]], row_sems.at[2 * index + half])
-
-        send_row(place.row, [0, 1], after, cot_ref)
-        send_row(place.row, [1, 0], before, cot_ref)
+        send_row(place.row, after, src=cot_ref)
+        send_row(place.row, before, src=cot_ref)
         yield
         for k in range(1, rows // 2):
             last = k == rows // 2 - 1
             low, high = (place.row + rows - k) % rows, (place.row + k) % rows
-            got_row(low, [0])
-            send_row(low, [0], after)
-            got_row(high, [1])
-            send_row(high, [1], before)
-            got_row(low, [1])
-            if not last:
-                send_row(low, [1], after)
-            got_row(high, [0])
-            if not last:
-                send_row(high, [0], before)
+            got_row(low)
+            send_row(low, after, 0 if last else None)
+            got_row(high)
+            send_row(high, before, 1 if last else None)
             yield
-        got_row((place.row + rows // 2) % rows, [0, 1])
-
-    run_in_order({"f": feats_pipe(), "c": cot_pipe()}, "fcfcffcffcff")
+        got_row((place.row + rows // 2) % rows, halves=True)
+
+    pair_iota = lax.broadcasted_iota(jnp.int32, (PAIR, EDGE_TILE), 0)
+    tile_iota = lax.broadcasted_iota(jnp.int32, (TILE, EDGE_TILE), 0)
+    edge_iota = lax.broadcasted_iota(jnp.int32, (1, EDGE_TILE), 1)
+    tile_copies = []
+
+    def tile(slot, _):
+        at = pl.ds(slot, 1)
+        edges = jnp.where(slot < live_ref[0], count_ref[slot], 0)
+        ends = ends_ref[at, :]
+        key = dir_ref[at, :] * TILE + lax.shift_right_logical(ends, 7)
+        hot_dst = hot(pair_iota, jnp.where(edge_iota < edges, key, NONE))
+        hot_src = hot(tile_iota, ends & (TILE - 1))
+        hot_rel = hot(pair_iota, relation_ref[at, :])
+        forward_ref[slot] = dot(hot_dst, hot_src, NT).astype(BF16)
+        backward_ref[slot] = dot(hot_src, hot_dst, NT).astype(BF16)
+        counted_ref[slot] = dot(hot_dst, hot_rel, NT).astype(BF16)
+        return 0
+
+    def tiles_pipe():
+        chunk = ends_ref.shape[0] // PREPARED
+        for part in range(PREPARED):
+            lax.fori_loop(part * chunk, (part + 1) * chunk, tile, 0, unroll=2)
+            here = pl.ds(part * chunk, chunk)
+            for which, (src, dst) in enumerate(
+                ((forward_ref, forward_any), (backward_ref, backward_any), (counted_ref, counted_any))
+            ):
+                copy = pltpu.make_async_copy(src.at[here], dst.at[here], tile_sems.at[3 * part + which])
+                copy.start()
+                tile_copies.append(copy)
+            yield
+
+    run_in_order({"f": feats_pipe(), "c": cot_pipe(), "p": tiles_pipe()}, "fcppppfpfcpfppcfppfpcfpppfppcff")
+    for copy in tile_copies:
+        copy.wait()
     for copy in own_copies:
         copy.wait()
     copies.finish()
 
 
-def gather_call(feats, cot, rows, cols):
+def gather_call(live, counts, ends, relation, direction, feats, cot, rows, cols):
     anywhere = pl.BlockSpec(memory_space=pl.ANY)
-    sources, targets = pl.pallas_call(
+    smem = pl.BlockSpec(memory_space=pltpu.SMEM)
+    vmem = pl.BlockSpec(memory_space=pltpu.VMEM)
+    slots = ends.shape[0]
+    shapes = [(slots, PAIR, TILE), (slots, TILE, PAIR), (slots, PAIR, RELS_PAD)]
+    sources, targets, *tiles = pl.pallas_call(
         functools.partial(gather_kernel, rows),
         out_shape=[
             jax.ShapeDtypeStruct((cols,) + feats.shape, feats.dtype),
             jax.ShapeDtypeStruct((rows,) + cot.shape, cot.dtype),
-        ],
-        in_specs=[anywhere] * 2,
-        out_specs=[anywhere] * 2,
-        scratch_shapes=[
-            pltpu.SemaphoreType.DMA((160,)),
-            pltpu.SemaphoreType.DMA((2 * cols,)),
-            pltpu.SemaphoreType.DMA((2 * rows,)),
+        ]
+        + [jax.ShapeDtypeStruct(shape, BF16) for shape in shapes],
+        in_specs=[smem] * 2 + [vmem] * 3 + [anywhere] * 2,
+        out_specs=[anywhere] * 5,
+        scratch_shapes=[pltpu.VMEM(shape, BF16) for shape in shapes]
+        + [
+            pltpu.SemaphoreType.DMA((64,)),
+            pltpu.SemaphoreType.DMA((3 * cols,)),
+            pltpu.SemaphoreType.DMA((3 * rows,)),
             pltpu.SemaphoreType.DMA((2,)),
+            pltpu.SemaphoreType.DMA((3 * PREPARED,)),
         ],
         compiler_params=pltpu.CompilerParams(
-            collective_id=0, has_side_effects=True, vmem_limit_bytes=VMEM_LIMIT
+            collective_id=0, has_side_effects=True, vmem_limit_bytes=GATHER_VMEM
         ),
         name="gather",
-    )(feats, cot)
-    return sources.reshape(-1, D), targets.reshape(-1, D)
+    )(live, counts, ends, relation, direction, feats, cot)
+    return [sources.reshape(-1, D), targets.reshape(-1, D)] + tiles
 
 
 def reduce_kernel(
@@ -771,7 +808,7 @@
             pltpu.SemaphoreType.DMA((16,)),
         ],
         compiler_params=pltpu.CompilerParams(
-            collective_id=1, has_side_effects=True, vmem_limit_bytes=48 * 1024 * 1024
+            collective_id=1, has_side_effects=True, vmem_limit_bytes=REDUCE_VMEM
         ),
         name="reduce",
     )(
@@ -795,22 +832,11 @@
     edge_dir,
     edge_count,
 ):
-    rows_n = lax.axis_size("row")
-    cols_n = lax.axis_size("col")
-    sources, targets = gather_call(feats, cot, rows_n, cols_n)
-    grad, mixed, sums = tiles_call(
-        tile_row,
-        tile_col,
-        tile_live,
-        edge_count,
-        edge_ends,
-        edge_relation,
-        edge_dir,
-        rel_embed,
-        weights,
-        sources,
-        targets,
+    rows_n, cols_n = lax.axis_size("row"), lax.axis_size("col")
+    sources, targets, *tiles = gather_call(
+        tile_live, edge_count, edge_ends, edge_relation, edge_dir, feats, cot, rows_n, cols_n
     )
+    grad, mixed, sums = tiles_call(tile_row, tile_col, rel_embed, weights, sources, targets, *tiles)
     rels_all = rel_embed.shape[0]
     grad_feats, mixed, sums = reduce_call(grad, mixed, sums, rows_n, cols_n)
     grad_rel = sums[3 * D : 3 * D + rels_all]

time: 115 us -> 113 us (0.983)
  local copies, waits for them, and re-layouts: 5.84 us -> 3.03 us
    pallas_call x1, Pallas kernels: 29.6 us -> 23.9 us  [tiles_call(): pl.pallas_call(tiles_kernel, out_shape=[jax.ShapeDtypeStruct((src_dev, D)...]
    pallas_call x1, Pallas kernels: 29.9 us -> 33.9 us  [gather_call(): pl.pallas_call(functools.partial(gather_kernel, rows), out_shape=[jax.Sha...]
    unnamed x6 -> x2, local copies, waits for them, and re-layouts: 4.21 us -> 1.4 us
    pallas_call x1, Pallas kernels: 48.1 us -> 50.5 us  [reduce_call(): pl.pallas_call(functools.partial(reduce_kernel, rows), out_shape=[jax.Sha...]
where the time goes in v4:
time: 113 us
  Pallas kernels  108 us (96%)
  local copies, waits for them, and re-layouts  3.03 us (3%)
  between operations  1.3 us (1%)
    pallas_call x1, Pallas kernels, reduce_call(): pl.pallas_call(functools.partial(reduce_kernel, rows), out_shape=[jax.Sha...  50.5 us
    pallas_call x1, Pallas kernels, gather_call(): pl.pallas_call(functools.partial(gather_kernel, rows), out_shape=[jax.Sha...  33.9 us
    pallas_call x1, Pallas kernels, tiles_call(): pl.pallas_call(tiles_kernel, out_shape=[jax.ShapeDtypeStruct((src_dev, D)...  23.9 us

profile of v4, /device:TPU:6, one launch (start us, length us, event | category | flops | bytes accessed | tf_op | source)
XLA Modules:
  0.0 112.6 jit_solution(5424743148325297543)
XLA Ops:
  1.3 33.9 %gather.1 = (bf16[32,256,256]{2,1,0:T(8,128)(2,1)}, bf16[8,256,256]{2,1,0:T(8,128)(2,1)}, bf16[64,256,128]{2,1,0:T(8,128)(2,1)}, bf16[64,128,256]{2,1,0:T(8,128)(2,1)}, bf16[64,256,256]{2,1,0:T(8,128)(2,1)}) custom-call(s32[1]{0:T(128)S(6)} %copy.17.live_ref, s32[64]{0:T(128)} %count_ref.1, s32[64,256]{1,0:T(8,128)} %ends_ref.1, s32[64,256]{1,0:T(8,128)} %relation_ref.1, ...), custom_call_target="tpu_custom_call" | custom-call | tf_op jit(solution)/shard_map/gather/pallas_call | solution.py:528
  35.2 23.9 %tiles.1 = (f32[8192,256]{1,0:T(8,128)}, f32[2048,256]{1,0:T(8,128)}, f32[1024,256]{1,0:T(8,128)}) custom-call(s32[64]{0:T(128)} %row_ref.1, s32[64]{0:T(128)} %col_ref.1, f32[201,256]{1,0:T(8,128)} %rel_ref.1, f32[3,256,256]{2,1,0:T(8,128)} %weights_ref.1, bf16[8192,256]{1,0:T(8,128)(2,1)} %bitcast.10, bf16[2048,256]{1,0:T(8,128)(2,1)} %bitcast.12, ...), custom_call_target="tpu_custom_call" | custom-call | tf_op jit(solution)/shard_map/tiles/pallas_call | solution.py:260
  59.1 50.5 %reduce.1 = (f32[256,256]{1,0:T(8,128)S(1)}, f32[256,256]{1,0:T(8,128)S(1)}, f32[2,4,4,32,256]{4,3,2,1,0:T(8,128)S(1)}) custom-call(f32[16,2,256,256]{3,2,1,0:T(8,128)} %bitcast.9, f32[8,256,256]{2,1,0:T(8,128)} %bitcast.11, f32[2,4,4,32,256]{4,3,2,1,0:T(8,128)} %bitcast.13), custom_call_target="tpu_custom_call" | custom-call | tf_op jit(solution)/shard_map/reduce/pallas_call | solution.py:777
  109.6 0.7 slice.8
  110.3 0.9 slice.9
  111.2 0.7 copy.18
  111.9 0.7 copy.19

commit v5 on v4

--- a/solution.py
+++ b/solution.py
@@ -83,6 +83,7 @@
     count_high_ref,
     grad_ref,
     self_rel_ref,
+    self_sum_ref,
     sems,
 ):
     slots = forward_ref.shape[0]
@@ -140,32 +141,31 @@
     @pl.when(owner)
     def _():
         def self_image(block, total):
-            image = dot_exact_left(cot_ref[rows_at(block, PAIR), :], weight[2], NT)
-            grad_ref[pl.ds(pl.multiple_of((ahead + 2 * block) * TILE, TILE), PAIR), :] = image
-            return total + jnp.sum(image.reshape(PAIR // 8, 8, D), axis=0)
-
-        self_rel_ref[...] = lax.fori_loop(0, blocks // 2, self_image, jnp.zeros((8, D), F32), unroll=2)
+            cot = cot_ref[rows_at(block, PAIR), :]
+            grad_ref[pl.ds(pl.multiple_of((ahead + 2 * block) * TILE, TILE), PAIR), :] = dot_exact_left(
+                cot, weight[2], NT
+            )
+            return total + jnp.sum(cot.astype(F32).reshape(PAIR // 8, 8, D), axis=0)
+
+        self_sum_ref[...] = lax.fori_loop(0, blocks // 2, self_image, jnp.zeros((8, D), F32), unroll=2)
 
     load_feats.wait()
 
     @pl.when(owner)
     def _():
-        own_rel = rel_ref[pl.ds(rels_all - 1, 1), :]
+        own_rel = split(jnp.broadcast_to(rel_ref[pl.ds(rels_all - 1, 1), :], (8, D)))
+        rel_image = dot_split(own_rel, weight[2])[:1]
 
         def self_block(block, _):
-            here = rows_at(block, PAIR)
             there = pl.ds(pl.multiple_of((ahead + 2 * block) * TILE, TILE), PAIR)
-            self_term = split(feats_ref[there, :].astype(F32) - own_rel)
-            count_high_ref[0, here, :] = self_term[0]
-            count_high_ref[1, here, :] = self_term[1]
-            mixed_ref[here, :] = dot_split(self_term, weight[2])
+            mixed_ref[rows_at(block, PAIR), :] = dot_exact_left(feats_ref[there, :], weight[2]) - rel_image
             return 0
 
         lax.fori_loop(0, blocks // 2, self_block, 0, unroll=2)
-        turned = turned_ref[...]
-        product = dot(turned, count_high_ref[0]) + dot(turned, count_high_ref[1])
-        sums_ref[pl.ds(2 * D, D), :] = product.T
-
+        there = pl.ds(pl.multiple_of(ahead * TILE, TILE), dst_dev)
+        own_sum = split(self_sum_ref[...])
+        sums_ref[pl.ds(2 * D, D), :] = dot(turned_ref[...], feats_ref[there, :]).T - dot_split(own_rel, own_sum, TN)
+        self_rel_ref[...] = dot_split(own_sum, weight[2], NT)
 
     def tile(slot, _):
         row = rows_at(row_ref[slot] % blocks, PAIR)
@@ -280,6 +280,7 @@
             pltpu.VMEM((2 * dst_dev, D), BF16),
             pltpu.VMEM((2, dst_dev, RELS_PAD), BF16),
             pltpu.VMEM((src_dev, D), F32),
+            pltpu.VMEM((8, D), F32),
             pltpu.VMEM((8, D), F32),
             pltpu.SemaphoreType.DMA((6 + 3 * CHUNKS,)),
         ],
@@ -763,7 +764,7 @@
 
     run_in_order(
         {"s": sums_pipe(), "m": mixed_pipe(), "g": grad_pipe()},
-        "smgsmgsmgsmgsmgsmgsmgsmgmg",
+        "sgmsgmsgmsgmsgmsgmsgmsgmgg",
     )
     copies.finish()
 
@@ -819,6 +820,37 @@
     return grad_out, mixed_out, sums_out.reshape(-1, D)
 
 
+def place_kernel(grad_in, mixed_in, sums_in, mixed_out, grad_out, grad_rel_out, grad_weights_out, rel_ref, sems):
+    rels_all = grad_rel_out.shape[0]
+    pairs = [(sums_in.at[pl.ds(3 * D, RELS_PAD)], rel_ref), (mixed_in, mixed_out), (grad_in, grad_out)]
+    pairs += [(sums_in.at[pl.ds(which * D, D)], grad_weights_out.at[which]) for which in range(3)]
+    started = [pltpu.make_async_copy(src, dst, sems.at[index]) for index, (src, dst) in enumerate(pairs)]
+    for copy in started:
+        copy.start()
+    started[0].wait()
+    grad_rel_out[...] = rel_ref[pl.ds(0, rels_all), :]
+    for copy in started[1:]:
+        copy.wait()
+
+
+def place_call(grad, mixed, sums, rels_all):
+    anywhere = pl.BlockSpec(memory_space=pl.ANY)
+    return pl.pallas_call(
+        place_kernel,
+        out_shape=[
+            jax.ShapeDtypeStruct(mixed.shape, F32),
+            jax.ShapeDtypeStruct(grad.shape, F32),
+            jax.ShapeDtypeStruct((rels_all, D), F32),
+            jax.ShapeDtypeStruct((3, D, D), F32),
+        ],
+        in_specs=[anywhere] * 3,
+        out_specs=[anywhere, anywhere, pl.BlockSpec(memory_space=pltpu.VMEM), anywhere],
+        scratch_shapes=[pltpu.VMEM((RELS_PAD, D), F32), pltpu.SemaphoreType.DMA((6,))],
+        compiler_params=pltpu.CompilerParams(vmem_limit_bytes=REDUCE_VMEM),
+        name="place",
+    )(grad, mixed, sums)
+
+
 def shards(
     feats,
     rel_embed,
@@ -837,10 +869,8 @@
         tile_live, edge_count, edge_ends, edge_relation, edge_dir, feats, cot, rows_n, cols_n
     )
     grad, mixed, sums = tiles_call(tile_row, tile_col, rel_embed, weights, sources, targets, *tiles)
-    rels_all = rel_embed.shape[0]
     grad_feats, mixed, sums = reduce_call(grad, mixed, sums, rows_n, cols_n)
-    grad_rel = sums[3 * D : 3 * D + rels_all]
-    return (mixed, grad_feats, grad_rel, sums[: 3 * D].reshape(3, D, D))
+    return place_call(grad_feats, mixed, sums, rel_embed.shape[0])
 
 
 def solution(mesh):

time: 113 us -> 108 us (0.956)
  local copies, waits for them, and re-layouts: 3.03 us -> 0 us
  Pallas kernels: 108 us -> 105 us
    pallas_call x1, Pallas kernels: 50.5 us -> 45.9 us  [reduce_call(): pl.pallas_call(functools.partial(reduce_kernel, rows), out_shape=[jax.Sha...]
    pallas_call x0 -> x1, Pallas kernels: none -> 1.8 us  [place_call(): pl.pallas_call(place_kernel, out_shape=[jax.ShapeDtypeStruct(mixed.shape,...]
    slice x2 -> x0, local copies, waits for them, and re-layouts: 1.63 us -> none  [the longest x1 0.93 us: shards(): return (mixed, grad_feats, grad_rel, sums[:3 * D].reshape(3, D, D))]
    unnamed x2 -> x0, local copies, waits for them, and re-layouts: 1.4 us -> none
where the time goes in v5:
time: 108 us; the launch traced here: 107 us
  Pallas kernels  105 us (97%)
  between operations  1.48 us (1%)
    pallas_call x1, Pallas kernels, reduce_call(): pl.pallas_call(functools.partial(reduce_kernel, rows), out_shape=[jax.Sha...  45.9 us
    pallas_call x1, Pallas kernels, gather_call(): pl.pallas_call(functools.partial(gather_kernel, rows), out_shape=[jax.Sha...  33.9 us
    pallas_call x1, Pallas kernels, tiles_call(): pl.pallas_call(tiles_kernel, out_shape=[jax.ShapeDtypeStruct((src_dev, D)...  23.9 us

profile of v5, /device:TPU:6, one launch (start us, length us, event | category | flops | bytes accessed | tf_op | source)
XLA Modules:
  0.0 106.9 jit_solution(17563397579194636)
XLA Ops:
  1.3 33.9 %gather.1 = (bf16[32,256,256]{2,1,0:T(8,128)(2,1)}, bf16[8,256,256]{2,1,0:T(8,128)(2,1)}, bf16[64,256,128]{2,1,0:T(8,128)(2,1)}, bf16[64,128,256]{2,1,0:T(8,128)(2,1)}, bf16[64,256,256]{2,1,0:T(8,128)(2,1)}) custom-call(s32[1]{0:T(128)S(6)} %copy.15.live_ref, s32[64]{0:T(128)} %count_ref.1, s32[64,256]{1,0:T(8,128)} %ends_ref.1, s32[64,256]{1,0:T(8,128)} %relation_ref.1, ...), custom_call_target="tpu_custom_call" | custom-call | tf_op jit(solution)/shard_map/gather/pallas_call | solution.py:529
  35.2 23.9 %tiles.1 = (f32[8192,256]{1,0:T(8,128)}, f32[2048,256]{1,0:T(8,128)}, f32[1024,256]{1,0:T(8,128)}) custom-call(s32[64]{0:T(128)} %row_ref.1, s32[64]{0:T(128)} %col_ref.1, f32[201,256]{1,0:T(8,128)} %rel_ref.1, f32[3,256,256]{2,1,0:T(8,128)} %weights_ref.1, bf16[8192,256]{1,0:T(8,128)(2,1)} %bitcast.8, bf16[2048,256]{1,0:T(8,128)(2,1)} %bitcast.10, ...), custom_call_target="tpu_custom_call" | custom-call | tf_op jit(solution)/shard_map/tiles/pallas_call | solution.py:260
  59.1 45.9 %reduce.1 = (f32[256,256]{1,0:T(8,128)S(1)}, f32[256,256]{1,0:T(8,128)S(1)}, f32[2,4,4,32,256]{4,3,2,1,0:T(8,128)S(1)}) custom-call(f32[16,2,256,256]{3,2,1,0:T(8,128)} %bitcast.7, f32[8,256,256]{2,1,0:T(8,128)} %bitcast.9, f32[2,4,4,32,256]{4,3,2,1,0:T(8,128)} %bitcast.11), custom_call_target="tpu_custom_call" | custom-call | tf_op jit(solution)/shard_map/reduce/pallas_call | solution.py:778
  105.0 1.8 %place.1 = (f32[256,256]{1,0:T(8,128)}, f32[256,256]{1,0:T(8,128)}, f32[201,256]{1,0:T(8,128)}, f32[3,256,256]{2,1,0:T(8,128)}) custom-call(f32[256,256]{1,0:T(8,128)S(1)} %get-tuple-element.23.grad_in, f32[256,256]{1,0:T(8,128)S(1)} %get-tuple-element.24.mixed_in, f32[1024,256]{1,0:T(8,128)S(1)} %bitcast.6), custom_call_target="tpu_custom_call" | custom-call | tf_op jit(solution)/shard_map/place/pallas_call | solution.py:838

commit v6 on v5

--- a/solution.py
+++ b/solution.py
@@ -13,7 +13,8 @@
 PAIR = 2 * TILE
 RELS_PAD = 256
 NONE = 1024
-CHUNKS = 8
+CHUNKS = 4
+WIDE = 512
 PREPARED = 16
 GATHER_VMEM = 60 * 1024 * 1024
 TILES_VMEM = 60 * 1024 * 1024
@@ -123,31 +124,33 @@
     load_cot.wait()
 
     def image_block(block, _):
-        cot = cot_ref[rows_at(block, TILE), :]
-        turned_ref[:, rows_at(block, TILE)] = cot.T
-        at = rows_at(block, PAIR)
+        here = rows_at(block, WIDE)
+        cot = cot_ref[here, :]
+        turned_ref[:, here] = cot.T
         for which in range(2):
             high, low = split(dot_exact_left(cot, weight[which], NT))
-            part = pl.ds(pl.multiple_of(block * PAIR + which * TILE, TILE), TILE)
-            high_ref[part, :] = high
-            low_ref[part, :] = low
-        totals_ref[at, :] = jnp.zeros((PAIR, D), F32)
-        counts_ref[at, :] = jnp.zeros((PAIR, RELS_PAD), F32)
-        mixed_ref[rows_at(block, TILE), :] = jnp.zeros((TILE, D), F32)
+            for sub in range(WIDE // TILE):
+                first = (block * (WIDE // TILE) + sub) * PAIR + which * TILE
+                part = pl.ds(pl.multiple_of(first, TILE), TILE)
+                high_ref[part, :] = high[sub * TILE : (sub + 1) * TILE]
+                low_ref[part, :] = low[sub * TILE : (sub + 1) * TILE]
+        totals_ref[rows_at(block, 2 * WIDE), :] = jnp.zeros((2 * WIDE, D), F32)
+        counts_ref[rows_at(block, 2 * WIDE), :] = jnp.zeros((2 * WIDE, RELS_PAD), F32)
+        mixed_ref[here, :] = jnp.zeros((WIDE, D), F32)
         return 0
 
-    lax.fori_loop(0, blocks, image_block, 0, unroll=2)
+    lax.fori_loop(0, dst_dev // WIDE, image_block, 0, unroll=True)
 
     @pl.when(owner)
     def _():
         def self_image(block, total):
-            cot = cot_ref[rows_at(block, PAIR), :]
-            grad_ref[pl.ds(pl.multiple_of((ahead + 2 * block) * TILE, TILE), PAIR), :] = dot_exact_left(
+            cot = cot_ref[rows_at(block, WIDE), :]
+            grad_ref[pl.ds(pl.multiple_of(ahead * TILE + block * WIDE, TILE), WIDE), :] = dot_exact_left(
                 cot, weight[2], NT
             )
-            return total + jnp.sum(cot.astype(F32).reshape(PAIR // 8, 8, D), axis=0)
-
-        self_sum_ref[...] = lax.fori_loop(0, blocks // 2, self_image, jnp.zeros((8, D), F32), unroll=2)
+            return total + jnp.sum(cot.astype(F32).reshape(WIDE // 8, 8, D), axis=0)
+
+        self_sum_ref[...] = lax.fori_loop(0, dst_dev // WIDE, self_image, jnp.zeros((8, D), F32), unroll=True)
 
     load_feats.wait()
 
@@ -157,11 +160,11 @@
         rel_image = dot_split(own_rel, weight[2])[:1]
 
         def self_block(block, _):
-            there = pl.ds(pl.multiple_of((ahead + 2 * block) * TILE, TILE), PAIR)
-            mixed_ref[rows_at(block, PAIR), :] = dot_exact_left(feats_ref[there, :], weight[2]) - rel_image
+            there = pl.ds(pl.multiple_of(ahead * TILE + block * WIDE, TILE), WIDE)
+            mixed_ref[rows_at(block, WIDE), :] = dot_exact_left(feats_ref[there, :], weight[2]) - rel_image
             return 0
 
-        lax.fori_loop(0, blocks // 2, self_block, 0, unroll=2)
+        lax.fori_loop(0, dst_dev // WIDE, self_block, 0, unroll=True)
         there = pl.ds(pl.multiple_of(ahead * TILE, TILE), dst_dev)
         own_sum = split(self_sum_ref[...])
         sums_ref[pl.ds(2 * D, D), :] = dot(turned_ref[...], feats_ref[there, :]).T - dot_split(own_rel, own_sum, TN)
@@ -207,21 +210,35 @@
 
         lax.fori_loop(0, blocks, low_block, 0)
 
-    def finish_block(block, _):
-        at = rows_at(block, PAIR)
-        here = rows_at(block, TILE)
+    def relate_block(block, _):
+        at = rows_at(block, WIDE)
         counts = counts_ref[at, :].astype(BF16)
         totals = totals_ref[at, :] - (dot(counts, relations[0]) + dot(counts, relations[1]))
-        pieces = [split(totals[:TILE]), split(totals[TILE:])]
+        high, low = split(totals)
+        for sub in range(WIDE // PAIR):
+            here = rows_at(block * (WIDE // PAIR) + sub, TILE)
+            for which in range(2):
+                first = sub * PAIR + which * TILE
+                there = pl.ds(
+                    pl.multiple_of(which * dst_dev + (block * (WIDE // PAIR) + sub) * TILE, TILE), TILE
+                )
+                high_ref[there, :] = high[first : first + TILE]
+                low_ref[there, :] = low[first : first + TILE]
+                count_high_ref[which, here, :] = counts[first : first + TILE]
+        return 0
+
+    lax.fori_loop(0, 2 * dst_dev // WIDE, relate_block, 0, unroll=True)
+
+    def mix_block(block, _):
+        here = rows_at(block, WIDE)
+        parts = []
         for which in range(2):
-            there = pl.ds(pl.multiple_of(which * dst_dev + block * TILE, TILE), TILE)
-            high_ref[there, :] = pieces[which][0]
-            low_ref[there, :] = pieces[which][1]
-            count_high_ref[which, here, :] = counts[which * TILE : (which + 1) * TILE]
-        mixed_ref[here, :] += dot_split(pieces[0], weight[0]) + dot_split(pieces[1], weight[1])
+            there = pl.ds(pl.multiple_of(which * dst_dev + block * WIDE, WIDE), WIDE)
+            parts.append(dot_split((high_ref[there, :], low_ref[there, :]), weight[which]))
+        mixed_ref[here, :] += parts[0] + parts[1]
         return 0
 
-    lax.fori_loop(0, blocks, finish_block, 0, unroll=4)
+    lax.fori_loop(0, dst_dev // WIDE, mix_block, 0, unroll=True)
 
     turned = turned_ref[...]
     grad_rel = jnp.zeros((D, RELS_PAD), F32)

time: 108 us -> 102 us (0.944)
  Pallas kernels: 105 us -> 99.6 us
    pallas_call x1, Pallas kernels: 23.9 us -> 19.7 us  [tiles_call(): pl.pallas_call(tiles_kernel, out_shape=[jax.ShapeDtypeStruct((src_dev, D)...]
    pallas_call x1, Pallas kernels: 45.9 us -> 44.2 us  [reduce_call(): pl.pallas_call(functools.partial(reduce_kernel, rows), out_shape=[jax.Sha...]
where the time goes in v6:
time: 102 us; the launch traced here: 101 us
  Pallas kernels  99.6 us (98%)
  between operations  1.48 us (1%)
    pallas_call x1, Pallas kernels, reduce_call(): pl.pallas_call(functools.partial(reduce_kernel, rows), out_shape=[jax.Sha...  44.2 us
    pallas_call x1, Pallas kernels, gather_call(): pl.pallas_call(functools.partial(gather_kernel, rows), out_shape=[jax.Sha...  33.9 us
    pallas_call x1, Pallas kernels, tiles_call(): pl.pallas_call(tiles_kernel, out_shape=[jax.ShapeDtypeStruct((src_dev, D)...  19.7 us

profile of v6, /device:TPU:6, one launch (start us, length us, event | category | flops | bytes accessed | tf_op | source)
XLA Modules:
  0.0 101.1 jit_solution(15259165516289403239)
XLA Ops:
  1.3 33.9 %gather.1 = (bf16[32,256,256]{2,1,0:T(8,128)(2,1)}, bf16[8,256,256]{2,1,0:T(8,128)(2,1)}, bf16[64,256,128]{2,1,0:T(8,128)(2,1)}, bf16[64,128,256]{2,1,0:T(8,128)(2,1)}, bf16[64,256,256]{2,1,0:T(8,128)(2,1)}) custom-call(s32[1]{0:T(128)S(6)} %copy.15.live_ref, s32[64]{0:T(128)} %count_ref.1, s32[64,256]{1,0:T(8,128)} %ends_ref.1, s32[64,256]{1,0:T(8,128)} %relation_ref.1, ...), custom_call_target="tpu_custom_call" | custom-call | tf_op jit(solution)/shard_map/gather/pallas_call | solution.py:546
  35.2 19.7 %tiles.1 = (f32[8192,256]{1,0:T(8,128)}, f32[2048,256]{1,0:T(8,128)}, f32[1024,256]{1,0:T(8,128)}) custom-call(s32[64]{0:T(128)} %row_ref.1, s32[64]{0:T(128)} %col_ref.1, f32[201,256]{1,0:T(8,128)} %rel_ref.1, f32[3,256,256]{2,1,0:T(8,128)} %weights_ref.1, bf16[8192,256]{1,0:T(8,128)(2,1)} %bitcast.8, bf16[2048,256]{1,0:T(8,128)(2,1)} %bitcast.10, ...), custom_call_target="tpu_custom_call" | custom-call | tf_op jit(solution)/shard_map/tiles/pallas_call | solution.py:277
  54.9 44.2 %reduce.1 = (f32[256,256]{1,0:T(8,128)S(1)}, f32[256,256]{1,0:T(8,128)S(1)}, f32[2,4,4,32,256]{4,3,2,1,0:T(8,128)S(1)}) custom-call(f32[16,2,256,256]{3,2,1,0:T(8,128)} %bitcast.7, f32[8,256,256]{2,1,0:T(8,128)} %bitcast.9, f32[2,4,4,32,256]{4,3,2,1,0:T(8,128)} %bitcast.11), custom_call_target="tpu_custom_call" | custom-call | tf_op jit(solution)/shard_map/reduce/pallas_call | solution.py:795
  99.1 1.8 %place.1 = (f32[256,256]{1,0:T(8,128)}, f32[256,256]{1,0:T(8,128)}, f32[201,256]{1,0:T(8,128)}, f32[3,256,256]{2,1,0:T(8,128)}) custom-call(f32[256,256]{1,0:T(8,128)S(1)} %get-tuple-element.23.grad_in, f32[256,256]{1,0:T(8,128)S(1)} %get-tuple-element.24.mixed_in, f32[1024,256]{1,0:T(8,128)S(1)} %bitcast.6), custom_call_target="tpu_custom_call" | custom-call | tf_op jit(solution)/shard_map/place/pallas_call | solution.py:855

commit v7 on v6

--- a/solution.py
+++ b/solution.py
@@ -618,7 +618,8 @@
             own_copies[k, r] = copy
     place.greet(
         [partner]
-        + [place.peer(k1, k2) for k1 in range(RING) for k2 in range(RING) if k1 or k2]
+        + [place.peer(k, 0) for k in (1, 2, 3)]
+        + [place.peer(0, k) for k in (1, 2, 3)]
         + [place.along_row(k, rows) for k in range(1, rows)]
     )
     low, high = pl.ds(0, HALF), pl.ds(HALF, HALF)

time: 102 us -> 101 us (level)
  Pallas kernels: 99.6 us -> 97.8 us
    pallas_call x1, Pallas kernels: 44.2 us -> 42.4 us  [reduce_call(): pl.pallas_call(functools.partial(reduce_kernel, rows), out_shape=[jax.Sha...]
where the time goes in v7:
time: 101 us; the launch traced here: 99.2 us
  Pallas kernels  97.8 us (97%)
  between operations  1.48 us (1%)
    pallas_call x1, Pallas kernels, reduce_call(): pl.pallas_call(functools.partial(reduce_kernel, rows), out_shape=[jax.Sha...  42.4 us
    pallas_call x1, Pallas kernels, gather_call(): pl.pallas_call(functools.partial(gather_kernel, rows), out_shape=[jax.Sha...  33.9 us
    pallas_call x1, Pallas kernels, tiles_call(): pl.pallas_call(tiles_kernel, out_shape=[jax.ShapeDtypeStruct((src_dev, D)...  19.7 us

profile of v7, /device:TPU:6, one launch (start us, length us, event | category | flops | bytes accessed | tf_op | source)
XLA Modules:
  0.0 99.2 jit_solution(13634824499064933)
XLA Ops:
  1.3 33.9 %gather.1 = (bf16[32,256,256]{2,1,0:T(8,128)(2,1)}, bf16[8,256,256]{2,1,0:T(8,128)(2,1)}, bf16[64,256,128]{2,1,0:T(8,128)(2,1)}, bf16[64,128,256]{2,1,0:T(8,128)(2,1)}, bf16[64,256,256]{2,1,0:T(8,128)(2,1)}) custom-call(s32[1]{0:T(128)S(6)} %copy.15.live_ref, s32[64]{0:T(128)} %count_ref.1, s32[64,256]{1,0:T(8,128)} %ends_ref.1, s32[64,256]{1,0:T(8,128)} %relation_ref.1, ...), custom_call_target="tpu_custom_call" | custom-call | tf_op jit(solution)/shard_map/gather/pallas_call | solution.py:546
  35.2 19.7 %tiles.1 = (f32[8192,256]{1,0:T(8,128)}, f32[2048,256]{1,0:T(8,128)}, f32[1024,256]{1,0:T(8,128)}) custom-call(s32[64]{0:T(128)} %row_ref.1, s32[64]{0:T(128)} %col_ref.1, f32[201,256]{1,0:T(8,128)} %rel_ref.1, f32[3,256,256]{2,1,0:T(8,128)} %weights_ref.1, bf16[8192,256]{1,0:T(8,128)(2,1)} %bitcast.8, bf16[2048,256]{1,0:T(8,128)(2,1)} %bitcast.10, ...), custom_call_target="tpu_custom_call" | custom-call | tf_op jit(solution)/shard_map/tiles/pallas_call | solution.py:277
  54.9 42.4 %reduce.1 = (f32[256,256]{1,0:T(8,128)S(1)}, f32[256,256]{1,0:T(8,128)S(1)}, f32[2,4,4,32,256]{4,3,2,1,0:T(8,128)S(1)}) custom-call(f32[16,2,256,256]{3,2,1,0:T(8,128)} %bitcast.7, f32[8,256,256]{2,1,0:T(8,128)} %bitcast.9, f32[2,4,4,32,256]{4,3,2,1,0:T(8,128)} %bitcast.11), custom_call_target="tpu_custom_call" | custom-call | tf_op jit(solution)/shard_map/reduce/pallas_call | solution.py:796
  97.3 1.8 %place.1 = (f32[256,256]{1,0:T(8,128)}, f32[256,256]{1,0:T(8,128)}, f32[201,256]{1,0:T(8,128)}, f32[3,256,256]{2,1,0:T(8,128)}) custom-call(f32[256,256]{1,0:T(8,128)S(1)} %get-tuple-element.23.grad_in, f32[256,256]{1,0:T(8,128)S(1)} %get-tuple-element.24.mixed_in, f32[1024,256]{1,0:T(8,128)S(1)} %bitcast.6), custom_call_target="tpu_custom_call" | custom-call | tf_op jit(solution)/shard_map/place/pallas_call | solution.py:856
